TPU v7x, 256 devices: a whole 4x4x8 slice. The times are simulated.
256 devices in a mesh: batch: 16 (over z_hi, y, core), dap: 16 (over z_lo, x).
Axes of the slice: x: 4, y: 4, z: 8 (z_hi: 2, z_lo: 4; z = z_hi * 4 + z_lo), core: 2. Of those that a mesh axis runs over, the one named last changes fastest.
Arguments:
- alignment: bfloat16 [32, 128, 256, 256], P('batch', 'dap'), may hold values from -6 to 6
- cotangent: bfloat16 [32, 128, 256, 256], P('batch', 'dap'), may hold values from -6 to 6
- query_weight: bfloat16 [256, 256], replicated, may hold values from -3 to 3
- key_weight: bfloat16 [256, 256], replicated, may hold values from -3 to 3
- value_weight: bfloat16 [256, 256], replicated, may hold values from -0.375 to 0.375
- gate_weight: bfloat16 [256, 256], replicated, may hold values from -0.375 to 0.375
- gate_bias: float32 [256], replicated, may hold values from -4 to 4
- out_weight: bfloat16 [256, 256], replicated, may hold values from -0.375 to 0.375
- out_bias: float32 [256], replicated, may hold values from -3 to 3
- ln_gain: float32 [256], replicated, may hold values from 0.1 to 1.9
- ln_bias: float32 [256], replicated, may hold values from -3 to 3
Outputs:
- updated: bfloat16 [32, 128, 256, 256], P('batch', 'dap')
- grad_alignment: bfloat16 [32, 128, 256, 256], P('batch', 'dap')
- grad_projections: float32 [4, 256, 256], replicated
- grad_output: float32 [256, 256], replicated
- grad_vectors: float32 [4, 256], replicated
All inputs are finite; a program needn't handle non-finite values.
Results may differ from a plain program's by a relative error of at most 0.012.
The roundings to bfloat16 on the way count: a program that leaves them out, or rounds other values in their place, can miss the bound.
Values may be sent and summed in bfloat16 or wider, within the bound.
No kernel may reach another device: no remote copies, remote signals or barrier semaphores. Data moves between devices by JAX's collectives and lax.ppermute only.
A program may use at most 128 MiB of HBM per device.

v0:
```python
import math

import jax
import jax.numpy as jnp
from jax import lax
from jax.sharding import PartitionSpec as P

C = 256
HEADS = 8
HDIM = 32
ROWS = 128
RES = 256
HD = 256


EPSILON = 1e-05


def contract(form, left, right):
    return jnp.einsum(form, left, right, preferred_element_type=jnp.float32)


def column_block(columns, upstream, params):
    (
        query_weight,
        key_weight,
        value_weight,
        gate_weight,
        gate_bias,
        out_weight,
        out_bias,
        ln_gain,
        ln_bias,
    ) = params
    row_count, col_count = (columns.shape[0], columns.shape[1])
    inputs = columns.astype(jnp.float32)
    centered = inputs - jnp.mean(inputs, axis=-1, keepdims=True)
    inv_std = lax.rsqrt(jnp.mean(centered * centered, axis=-1, keepdims=True) + EPSILON)
    standard = centered * inv_std
    normed = (standard * ln_gain + ln_bias).astype(jnp.bfloat16)
    in_weights = jnp.concatenate([query_weight, key_weight, value_weight, gate_weight], axis=1)
    projected = contract("irc,cf->irf", normed, in_weights)
    inv_scale = 1.0 / math.sqrt(HDIM)
    split_shape = (row_count, col_count, HEADS, HDIM)
    queries = (projected[..., :HD] * inv_scale).astype(jnp.bfloat16).reshape(split_shape)
    key_rows = projected[..., HD : 2 * HD].astype(jnp.bfloat16).reshape(split_shape)
    value_rows = projected[..., 2 * HD : 3 * HD].astype(jnp.bfloat16).reshape(split_shape)
    gate_open = jax.nn.sigmoid(projected[..., 3 * HD :] + gate_bias)
    scores = contract("irhd,jrhd->rhij", queries, key_rows)
    shifted = jnp.exp(scores - jnp.max(scores, axis=-1, keepdims=True))
    soft = shifted / jnp.sum(shifted, axis=-1, keepdims=True)
    soft_half = soft.astype(jnp.bfloat16)
    attended = contract("rhij,jrhd->irhd", soft_half, value_rows).reshape(row_count, col_count, HD)
    gated = (gate_open * attended).astype(jnp.bfloat16)
    update = contract("irf,fc->irc", gated, out_weight) + out_bias
    updated = (inputs + update).astype(jnp.bfloat16)
    d_gated = contract("irc,fc->irf", upstream, out_weight)
    d_attended = (d_gated * gate_open).astype(jnp.bfloat16).reshape(split_shape)
    d_logit = (d_gated * attended * gate_open * (1.0 - gate_open)).astype(jnp.bfloat16)
    d_soft = contract("irhd,jrhd->rhij", d_attended, value_rows)
    d_scores = (soft * (d_soft - jnp.sum(soft * d_soft, axis=-1, keepdims=True))).astype(
        jnp.bfloat16
    )
    d_queries = (contract("rhij,jrhd->irhd", d_scores, key_rows) * inv_scale).astype(jnp.bfloat16)
    d_keys = contract("rhij,irhd->jrhd", d_scores, queries).astype(jnp.bfloat16)
    d_values = contract("rhij,irhd->jrhd", soft_half, d_attended).astype(jnp.bfloat16)
    flat_shape = (row_count, col_count, HD)
    d_projected = jnp.concatenate(
        [
            d_queries.reshape(flat_shape),
            d_keys.reshape(flat_shape),
            d_values.reshape(flat_shape),
            d_logit,
        ],
        axis=-1,
    )
    d_normed = contract("irf,cf->irc", d_projected, in_weights)
    grad_in = contract("irc,irf->cf", normed, d_projected).reshape(C, 4, HD).transpose(1, 0, 2)
    grad_out = contract("irf,irc->fc", gated, upstream)
    d_hat = d_normed * ln_gain
    branch = inv_std * (
        d_hat
        - jnp.mean(d_hat, axis=-1, keepdims=True)
        - standard * jnp.mean(d_hat * standard, axis=-1, keepdims=True)
    )
    grad_cols = (upstream.astype(jnp.float32) + branch).astype(jnp.bfloat16)
    vectors = jnp.stack(
        [
            jnp.sum(d_logit.astype(jnp.float32), axis=(0, 1)),
            jnp.sum(upstream.astype(jnp.float32), axis=(0, 1)),
            jnp.sum(d_normed * standard, axis=(0, 1)),
            jnp.sum(d_normed, axis=(0, 1)),
        ]
    )
    return (updated, grad_cols, grad_in, grad_out, vectors)


def shards(
    alignment,
    cotangent,
    query_weight,
    key_weight,
    value_weight,
    gate_weight,
    gate_bias,
    out_weight,
    out_bias,
    ln_gain,
    ln_bias,
):
    params = (
        query_weight,
        key_weight,
        value_weight,
        gate_weight,
        gate_bias,
        out_weight,
        out_bias,
        ln_gain,
        ln_bias,
    )
    columns, upstream = (
        lax.all_to_all(alignment, "dap", split_axis=2, concat_axis=1, tiled=True),
        lax.all_to_all(cotangent, "dap", split_axis=2, concat_axis=1, tiled=True),
    )
    new_cols, grad_cols, part_in, part_out, part_vec = lax.map(
        lambda pair: column_block(pair[0], pair[1], params), (columns, upstream)
    )
    updated, grad_alignment = (
        lax.all_to_all(new_cols, "dap", split_axis=1, concat_axis=2, tiled=True),
        lax.all_to_all(grad_cols, "dap", split_axis=1, concat_axis=2, tiled=True),
    )
    local_sums = (jnp.sum(part_in, axis=0), jnp.sum(part_out, axis=0), jnp.sum(part_vec, axis=0))
    totals = lax.psum((local_sums[0], local_sums[1], local_sums[2]), ("batch", "dap"))
    factor = 1.0 / math.sqrt(alignment.shape[0] * lax.axis_size("batch") * ROWS * RES)
    return (updated, grad_alignment, totals[0] * factor, totals[1] * factor, totals[2] * factor)


def solution(mesh):
    return jax.shard_map(
        shards,
        mesh=mesh,
        in_specs=(
            P("batch", "dap", None, None),
            P("batch", "dap", None, None),
            P(),
            P(),
            P(),
            P(),
            P(),
            P(),
            P(),
            P(),
            P(),
        ),
        out_specs=(P("batch", "dap", None, None), P("batch", "dap", None, None), P(), P(), P()),
        check_vma=False,
    )
```

profile of v0, /device:TPU:32, one launch (start us, length us, event | category | flops | bytes accessed | tf_op | source)
XLA Modules:
  0.0 630.9 jit_solution(8647443670775439200)
XLA Ops:
  7.2 4.1 copy.77
  11.2 8.5 %all-to-all-start.1 = ((bf16[2,8,256,256]{3,1,0,2:T(8,128)(2,1)}), bf16[2,8,256,256]{3,1,0,2:T(8,128)(2,1)S(1)}, u32[]{:S(2)}, u32[]{:S(2)}) async-start(bf16[2,8,256,256]{3,1,0,2:T(8,128)(2,1)} %copy.77), calls=%async_computation.1 | async-start | bytes 4194304 | tf_op jit(solution)/shard_map/all_to_all | solution.py:124
  19.7 4.1 copy.75
  23.8 43.2 %all-to-all-done.1 = bf16[2,8,256,256]{3,1,0,2:T(8,128)(2,1)S(1)} async-done(((bf16[2,8,256,256]{3,1,0,2:T(8,128)(2,1)}), bf16[2,8,256,256]{3,1,0,2:T(8,128)(2,1)S(1)}, u32[]{:S(2)}, u32[]{:S(2)}) %all-to-all-start.1) | async-done | bytes 2097184 | tf_op jit(solution)/shard_map/all_to_all | solution.py:124
  67.0 6.1 all-to-all-start
  74.9 44.7 %all-to-all-done = bf16[2,8,256,256]{3,1,0,2:T(8,128)(2,1)} async-done(((bf16[2,8,256,256]{3,1,0,2:T(8,128)(2,1)}), bf16[2,8,256,256]{3,1,0,2:T(8,128)(2,1)}, u32[]{:S(2)}, u32[]{:S(2)}) %all-to-all-start) | async-done | bytes 2097184 | tf_op jit(solution)/shard_map/all_to_all | solution.py:123
  121.5 170.0 %while.20 = (s32[]{:T(128)}, bf16[2,128,16,256]{3,2,0,1:T(8,128)(2,1)}, bf16[2,128,16,256]{3,2,0,1:T(8,128)(2,1)}, f32[2,4,256,256]{3,2,1,0:T(8,128)}, f32[2,256...) while((s32[]{:T(128)}, ...), condition=%wide.region_12.13_spmd, body=%wide.region_0.12_spmd.sunk | while | flops 4912041984 | bytes 300039360 | solution.py:126
  122.8 4.1 fusion.144
  130.0 2.8 fusion.146
  135.2 7.4 %fusion.147 = (f32[16,8,128]{2,1,0:T(8,128)S(1)}, f32[16,8,128,128]{2,3,1,0:T(8,128)}) fusion(bf16[128,16,8,32]{0,3,2,1:T(8,128)(2,1)} %bitcast.250, bf16[128,16,8,32]{0,3,2,1:T(8,128)(2,1)S(1)} %bitcast.248), kind=kOutput, calls=%fused_computation.103.clone.1 | convolution fusion | flops 138412160 | bytes 10551296 | tf_op jit(solution)/shard_map/while/body/eval_jaxpr/sub | solution.py:50
  144.8 6.3 fusion.148
  151.0 2.9 copy.125
  154.0 5.4 convert_reduce_fusion.7
  161.6 6.0 multiply_reduce_fusion.3
  175.5 5.5 convolution_convert_fusion.2
  183.3 6.7 %fusion.149 = bf16[16,8,32,128]{3,2,1,0:T(8,128)(2,1)} fusion(bf16[128,16,8,32]{0,3,2,1:T(8,128)(2,1)S(1)} %bitcast.258, f32[16,8,128,128]{2,3,1,0:T(8,128)} %get-tuple-element.359, f32[16,8,128]{2,1,0:T(8,128)S(1)} %get-tuple-element.360), kind=kOutput, calls=%fused_computation.52.clone.1 | convolution fusion | flops 138936320 | bytes 10551296 | tf_op jit(solution)/shard_map/while/body/eval_jaxpr/rhij,irhd->jrhd/dot_general | solution.py:20
  194.5 2.9 fusion.150
  207.7 4.1 fusion.144
  214.9 2.8 fusion.146
  220.0 7.4 %fusion.147 = (f32[16,8,128]{2,1,0:T(8,128)S(1)}, f32[16,8,128,128]{2,3,1,0:T(8,128)}) fusion(bf16[128,16,8,32]{0,3,2,1:T(8,128)(2,1)} %bitcast.250, bf16[128,16,8,32]{0,3,2,1:T(8,128)(2,1)S(1)} %bitcast.248), kind=kOutput, calls=%fused_computation.103.clone.1 | convolution fusion | flops 138412160 | bytes 10551296 | tf_op jit(solution)/shard_map/while/body/eval_jaxpr/sub | solution.py:50
  229.7 6.3 fusion.148
  235.9 2.9 copy.125
  238.8 5.4 convert_reduce_fusion.7
  246.5 6.0 multiply_reduce_fusion.3
  260.4 5.5 convolution_convert_fusion.2
  268.2 6.7 %fusion.149 = bf16[16,8,32,128]{3,2,1,0:T(8,128)(2,1)} fusion(bf16[128,16,8,32]{0,3,2,1:T(8,128)(2,1)S(1)} %bitcast.258, f32[16,8,128,128]{2,3,1,0:T(8,128)} %get-tuple-element.359, f32[16,8,128]{2,1,0:T(8,128)S(1)} %get-tuple-element.360), kind=kOutput, calls=%fused_computation.52.clone.1 | convolution fusion | flops 138936320 | bytes 10551296 | tf_op jit(solution)/shard_map/while/body/eval_jaxpr/rhij,irhd->jrhd/dot_general | solution.py:20
  279.4 2.9 fusion.150
  291.5 53.9 %all_to_all.72 = bf16[2,128,16,256]{3,2,0,1:T(8,128)(2,1)} all-to-all(bf16[2,128,16,256]{3,2,0,1:T(8,128)(2,1)} %get-tuple-element.193), channel_id=1, replica_groups=mesh['batch'=16,'dap'=16] {'dap'}, dimensions={1} | all-to-all | bytes 4194304 | tf_op jit(solution)/shard_map/all_to_all | solution.py:130
  345.4 5.1 all-to-all-start.3
  350.6 2.9 reduce_sum.137
  354.2 89.2 %psum.23 = f32[4,256]{1,0:T(4,128)S(1)} all-reduce(f32[4,256]{1,0:T(4,128)S(1)} %reduce_sum.139), channel_id=1, replica_groups=mesh['batch'=16,'dap'=16] {'batch','dap'}, use_global_device_ids=true, to_apply=%region_18.19 | all-reduce | flops 1024 | bytes 8192 | tf_op jit(solution)/shard_map/psum | solution.py:134
  444.0 172.9 %all-reduce.3.cloned.1.call-done = (f32[4,256,256]{2,1,0:T(8,128)}, f32[256,256]{1,0:T(8,128)}) async-done(((f32[4,256,256]{2,1,0:T(8,128)}, f32[256,256]{1,0:T(8,128)}), (f32[4,256,256]{2,1,0:T(8,128)}, f32[256,256]{1,0:T(8,128)})) %all-reduce.3.cloned.1.call-update) | async-done | bytes 1310736 | tf_op jit(solution)/shard_map/psum | solution.py:134
  (160 shorter events, 81.8 us)
Async XLA Ops:
  11.2 55.8 %all-to-all-start.1 = ((bf16[2,8,256,256]{3,1,0,2:T(8,128)(2,1)}), bf16[2,8,256,256]{3,1,0,2:T(8,128)(2,1)S(1)}, u32[]{:S(2)}, u32[]{:S(2)}) async-start(bf16[2,8,256,256]{3,1,0,2:T(8,128)(2,1)} %copy.77), calls=%async_computation.1 | async-start | bytes 4194304 | tf_op jit(solution)/shard_map/all_to_all | solution.py:124
  23.8 49.4 %copy-start.19 = (bf16[256,256]{1,0:T(8,128)(2,1)S(1)}, bf16[256,256]{1,0:T(8,128)(2,1)}, u32[]{:S(2)}) copy-start(bf16[256,256]{1,0:T(8,128)(2,1)} %param.18) | copy-start | bytes 393220
  23.8 49.4 %copy-start.20 = (bf16[256,256]{1,0:T(8,128)(2,1)S(1)}, bf16[256,256]{1,0:T(8,128)(2,1)}, u32[]{:S(2)}) copy-start(bf16[256,256]{1,0:T(8,128)(2,1)} %param.17) | copy-start | bytes 393220
  23.8 49.4 %copy-start.21 = (bf16[256,256]{1,0:T(8,128)(2,1)S(1)}, bf16[256,256]{1,0:T(8,128)(2,1)}, u32[]{:S(2)}) copy-start(bf16[256,256]{1,0:T(8,128)(2,1)} %param.16) | copy-start | bytes 393220
  23.8 49.4 %copy-start.22 = (bf16[256,256]{1,0:T(8,128)(2,1)S(1)}, bf16[256,256]{1,0:T(8,128)(2,1)}, u32[]{:S(2)}) copy-start(bf16[256,256]{1,0:T(8,128)(2,1)} %param.15) | copy-start | bytes 393220
  67.0 52.6 %all-to-all-start = ((bf16[2,8,256,256]{3,1,0,2:T(8,128)(2,1)}), bf16[2,8,256,256]{3,1,0,2:T(8,128)(2,1)}, u32[]{:S(2)}, u32[]{:S(2)}) async-start(bf16[2,8,256,256]{3,1,0,2:T(8,128)(2,1)} %copy.75), calls=%async_computation | async-start | bytes 4194304 | tf_op jit(solution)/shard_map/all_to_all | solution.py:123
  121.7 5.1 copy-start.6
  161.6 6.0 slice-start
  161.6 6.5 %slice-start.1 = ((s8[8388608]{0:T(1024)(128)(4,1)}), s8[4194304]{0:T(1024)(128)(4,1)S(1)}, s32[]{:S(2)}) async-start(s8[8388608]{0:T(1024)(128)(4,1)} %bitcast.245), calls=%async_computation.6 | async-start | bytes 8388608 | tf_op jit(solution)/shard_map/while
  170.8 2.4 copy-start
  173.1 2.3 copy-start.1
  180.9 2.4 copy-start.5
  190.0 2.4 copy-start.3
  194.5 3.0 copy-start.4
  201.9 2.0 copy-start.11
  202.2 3.2 copy-start.16
  204.0 2.6 copy-start.7
  206.6 5.1 copy-start.6
  246.5 6.0 slice-start
  246.5 6.5 %slice-start.1 = ((s8[8388608]{0:T(1024)(128)(4,1)}), s8[4194304]{0:T(1024)(128)(4,1)S(1)}, s32[]{:S(2)}) async-start(s8[8388608]{0:T(1024)(128)(4,1)} %bitcast.245), calls=%async_computation.6 | async-start | bytes 8388608 | tf_op jit(solution)/shard_map/while
  255.7 2.4 copy-start
  258.0 2.3 copy-start.1
  265.8 2.4 copy-start.5
  274.9 2.4 copy-start.3
  279.4 3.0 copy-start.4
  286.8 2.0 copy-start.11
  287.1 3.2 copy-start.16
  288.9 2.6 copy-start.7
  345.4 277.1 %all-to-all-start.3 = ((bf16[2,128,16,256]{3,2,0,1:T(8,128)(2,1)}), bf16[2,128,16,256]{3,2,0,1:T(8,128)(2,1)S(1)}, u32[]{:S(2)}, u32[]{:S(2)}) async-start(bf16[2,128,16,256]{3,2,0,1:T(8,128)(2,1)} %get-tuple-element.194), calls=%async_computation.3 | async-start | bytes 4194304 | tf_op jit(solution)/shard_map/all_to_all | solution.py:131
  350.5 2.9 copy-start.18
  350.5 266.3 %all-reduce.3.cloned.1.call-start = ((), (), s32[]{:S(2)}) async-start(), calls=%async_computation.4 | async-start | bytes 2621440 | tf_op jit(solution)/shard_map/psum | solution.py:134
  616.9 4.1 copy-start.8
  (19 other events, 31.2 us)
Sparse Core Ops, SparseCore 0:
  357.4 259.4 all-reduce.2
where the time goes:
time: 635 us; the launch traced here: 631 us
  waiting for transfers between devices  261 us (41%)
  blocking collectives  143 us (23%)
  matrix products  98.4 us (15%)
  local copies, waits for them, and re-layouts  65.7 us (10%)
  other arithmetic  28.3 us (4%)
  starting transfers between devices  19.7 us (3%)
  between operations  14.2 us (2%)
    psum x1, waiting for transfers between devices, shards(): lax.psum((local_sums[0], local_sums[1], local_sums[2]), ('batch', 'dap'))  173 us
    psum x1, blocking collectives, shards(): lax.psum((local_sums[0], local_sums[1], local_sums[2]), ('batch', 'dap'))  89.2 us
    dot_general x22, matrix products, contract(): return jnp.einsum(form, left, right, preferred_element_type=jnp.float32)  83.6 us
    all_to_all x1, blocking collectives, shards(): lax.all_to_all(new_cols, 'dap', split_axis=1, concat_axis=2, tiled=True)  53.9 us
    all_to_all x1, waiting for transfers between devices, shards(): lax.all_to_all(alignment, 'dap', split_axis=2, concat_axis=1, tiled=True)  44.7 us
    all_to_all x1, waiting for transfers between devices, shards(): lax.all_to_all(cotangent, 'dap', split_axis=2, concat_axis=1, tiled=True)  43.2 us
    sub x2, matrix products, column_block(): shifted = jnp.exp(scores - jnp.max(scores, axis=-1, keepdims=True))  14.7 us
  transfers between devices with their start and end apart: 4, of which 3 were waited for; matrix products, arithmetic and copies ran while one was open for 2% of the time, Pallas kernels for 0%

commit v1 on v0

v1 whole, which is shorter than its diff:
```python
import functools
import math

import jax
import jax.numpy as jnp
from jax import lax
from jax.experimental import pallas as pl
from jax.experimental.pallas import tpu as pltpu
from jax.sharding import Mesh
from jax.sharding import PartitionSpec as P

C = 256
HEADS = 8
HDIM = 32
ROWS = 128
RES = 256
HD = 256
STRUCTS = 32
EPSILON = 1e-05
INV_SCALE = 1.0 / math.sqrt(HDIM)
FACTOR = 1.0 / math.sqrt(STRUCTS * ROWS * RES)
F32 = jnp.float32
BF16 = jnp.bfloat16

MEMBERS = 16
OWN_ROWS = ROWS // MEMBERS
OWN_RES = RES // MEMBERS
PAIRS = OWN_RES // 2
DAP = ("z_lo", "x")
BATCH = ("z_hi", "y", "core")
RING = ("z_hi", "z_lo")
TILES = 352
GROUP = 4


def dot(left, right, left_dim=1, right_dim=0):
    return lax.dot_general(
        left, right, (((left_dim,), (right_dim,)), ((), ())), preferred_element_type=F32
    )


def pack_kernel(x_ref, cot_ref, out_ref, wide):
    count = GROUP * OWN_RES
    for which, ref in enumerate((x_ref, cot_ref)):
        for row in range(OWN_ROWS):
            for side in range(2):
                wide[side, pl.ds(row, count, stride=OWN_ROWS), :] = ref[
                    0, row, :, side * 128 : side * 128 + 128
                ].astype(F32)
        for side in range(2):
            out_ref[:, which, :, :, side * 128 : side * 128 + 128] = (
                wide[side].reshape(GROUP, PAIRS, 16, 128).astype(BF16)
            )


def pack(alignment, cotangent, struct):
    block = pl.BlockSpec((1, OWN_ROWS, GROUP * OWN_RES, C), lambda g: (struct, 0, g, 0))
    return pl.pallas_call(
        pack_kernel,
        grid=(MEMBERS // GROUP,),
        in_specs=[block, block],
        out_specs=pl.BlockSpec((GROUP, 2, PAIRS, 16, C), lambda g: (g, 0, 0, 0, 0)),
        out_shape=jax.ShapeDtypeStruct((MEMBERS, 2, PAIRS, 16, C), BF16),
        scratch_shapes=[pltpu.VMEM((2, GROUP * OWN_RES * OWN_ROWS, 128), F32)],
        compiler_params=pltpu.CompilerParams(vmem_limit_bytes=16 * 2**20),
        cost_estimate=pl.CostEstimate(flops=0, bytes_accessed=2**22, transcendentals=0),
    )(alignment, cotangent)


def unpack_kernel(*refs):
    in_ref, upd_ref, grad_ref, wide = refs[0], *refs[-3:]
    count = GROUP * OWN_RES
    for which, ref in enumerate((upd_ref, grad_ref)):
        for side in range(2):
            lanes = slice(side * 128, side * 128 + 128)
            wide[side] = in_ref[:, which, :, :, lanes].astype(F32).reshape(count * OWN_ROWS, 128)
            for row in range(OWN_ROWS):
                ref[0, row, :, lanes] = wide[
                    side, pl.ds(row, count, stride=OWN_ROWS), :
                ].astype(BF16)


def unpack(packed, struct, structs, earlier):
    block = pl.BlockSpec((1, OWN_ROWS, GROUP * OWN_RES, C), lambda g: (struct, 0, g, 0))
    shape = jax.ShapeDtypeStruct((structs, OWN_ROWS, RES, C), BF16)
    return pl.pallas_call(
        unpack_kernel,
        grid=(MEMBERS // GROUP,),
        in_specs=[pl.BlockSpec((GROUP, 2, PAIRS, 16, C), lambda g: (g, 0, 0, 0, 0))]
        + [pl.BlockSpec(memory_space=pl.ANY)] * len(earlier),
        out_specs=[block, block],
        out_shape=[shape, shape],
        input_output_aliases={1 + k: k for k in range(len(earlier))},
        scratch_shapes=[pltpu.VMEM((2, GROUP * OWN_RES * OWN_ROWS, 128), F32)],
        compiler_params=pltpu.CompilerParams(vmem_limit_bytes=16 * 2**20),
        cost_estimate=pl.CostEstimate(flops=0, bytes_accessed=2**22, transcendentals=0),
    )(packed, *earlier)


def token_rows(block):
    wide = block.astype(F32)
    return jnp.concatenate([wide[:, :8].reshape(ROWS, C), wide[:, 8:].reshape(ROWS, C)], axis=0)


def row_blocks(tokens):
    return jnp.concatenate(
        [tokens[:ROWS].reshape(MEMBERS, 8, C), tokens[ROWS:].reshape(MEMBERS, 8, C)], axis=1
    )


def fold_rows(tokens):
    return jnp.sum(tokens.reshape(tokens.shape[0] // 8, 8, C), axis=0)


def tiles_of(matrix):
    count = matrix.shape[0] // 8
    return matrix[:, :128].reshape(count, 8, 128), matrix[:, 128:].reshape(count, 8, 128)


def pair_kernel(steps, has_earlier, *refs):
    x_ref, cot_ref, w_ref, wt_ref, wo_ref, gb_ref, rows_ref = refs[:7]
    out_ref, sums_ref, qc, kc, vc, dac, attc, dprojc, gin, gout, vec, dlog = refs[-12:]

    @pl.when(pl.program_id(0) == 0)
    def _():
        gin[...] = jnp.zeros_like(gin)
        gout[...] = jnp.zeros_like(gout)
        vec[...] = jnp.zeros_like(vec)
        dlog[...] = jnp.zeros_like(dlog)

    out_bias, gain, bias = rows_ref[0:1], rows_ref[1:2], rows_ref[2:3]
    x = token_rows(x_ref[:, 0, 0])
    cot = token_rows(cot_ref[:, 0, 0])
    cot_half = cot.astype(BF16)
    centered = x - jnp.mean(x, axis=-1, keepdims=True)
    inv_std = lax.rsqrt(jnp.mean(centered * centered, axis=-1, keepdims=True) + EPSILON)
    standard = centered * inv_std
    normed = (standard * gain + bias).astype(BF16)

    kv = dot(normed, w_ref[:, HD : 3 * HD]).astype(BF16)
    proj = dot(wt_ref[...], normed, 1, 1)
    qc[...] = (proj[:HD] * INV_SCALE).astype(BF16)
    kc[...] = proj[HD : 2 * HD].astype(BF16)
    vc[...] = proj[2 * HD : 3 * HD].astype(BF16)
    gate = jax.nn.sigmoid(proj[3 * HD :] + jnp.concatenate([gb_ref[...]] * 2, axis=1))
    d_gated = dot(wo_ref[...], cot_half, 1, 1)
    dac[...] = (d_gated * gate).astype(BF16)

    head_of_lane = lax.broadcasted_iota(jnp.int32, (1, 128), 1) // HDIM
    for r in range(2):
        toks = slice(r * ROWS, (r + 1) * ROWS)
        for half in range(2):
            lanes = slice(half * 128, half * 128 + 128)
            k_half = kv[toks, half * 128 : half * 128 + 128]
            v_half = kv[toks, HD + half * 128 : HD + half * 128 + 128]
            zero = jnp.zeros_like(k_half)
            k_stack = jnp.concatenate(
                [jnp.where(head_of_lane == h, k_half, zero) for h in range(4)], axis=0
            )
            v_stack = jnp.concatenate(
                [jnp.where(head_of_lane == h, v_half, zero) for h in range(4)], axis=0
            )
            scores = dot(k_stack, qc[lanes, toks])
            d_softs = dot(v_stack, dac[lanes, toks])
            for h in range(4):
                s = scores[h * 128 : h * 128 + 128]
                shifted = jnp.exp(s - jnp.max(s, axis=0, keepdims=True))
                soft = shifted * (1.0 / jnp.sum(shifted, axis=0, keepdims=True))
                soft_half = soft.astype(BF16)
                weighted = soft * d_softs[h * 128 : h * 128 + 128]
                d_s = (weighted - soft * jnp.sum(weighted, axis=0, keepdims=True)).astype(BF16)
                f = half * 128 + h * HDIM
                chans = slice(f, f + HDIM)
                attc[chans, toks] = dot(vc[chans, toks], soft_half)
                dprojc[chans, toks] = (dot(kc[chans, toks], d_s) * INV_SCALE).astype(BF16)
                dprojc[HD + f : HD + f + HDIM, toks] = dot(qc[chans, toks], d_s, 1, 1).astype(BF16)
                dprojc[2 * HD + f : 2 * HD + f + HDIM, toks] = dot(
                    dac[chans, toks], soft_half, 1, 1
                ).astype(BF16)

    gated = gate * attc[...]
    d_logit = (d_gated * gated * (1.0 - gate)).astype(BF16)
    dprojc[3 * HD :, :] = d_logit
    gated_half = gated.astype(BF16)
    dlog[...] += d_logit.astype(F32)[:, :128] + d_logit.astype(F32)[:, 128:]
    gin[...] += dot(dprojc[...], normed)
    gout[...] += dot(gated_half, cot_half)
    update = dot(gated_half.T, wo_ref[...]) + out_bias
    out_ref[:, 0, 0] = row_blocks(x + update).astype(BF16)
    d_normed = dot(w_ref[...], dprojc[...]).T
    d_hat = d_normed * gain
    d_std = d_normed * standard
    branch = inv_std * (
        d_hat
        - jnp.mean(d_hat, axis=-1, keepdims=True)
        - standard * jnp.mean(d_hat * standard, axis=-1, keepdims=True)
    )
    out_ref[:, 1, 0] = row_blocks(cot + branch).astype(BF16)
    vec[0] += fold_rows(cot)
    vec[1] += fold_rows(d_std)
    vec[2] += fold_rows(d_normed)

    @pl.when(pl.program_id(0) == steps - 1)
    def _():
        def put(first, tiles):
            count = tiles.shape[0]
            if has_earlier:
                tiles = tiles + refs[7][first : first + count]
            sums_ref[first : first + count] = tiles

        for block in range(5):
            matrix = gin[block * HD : (block + 1) * HD].T if block < 4 else gout[...]
            left, right = tiles_of(matrix)
            put(block * 32, left)
            put(160 + block * 32, right)
        rows = [jnp.sum(dlog[...].T, axis=0, keepdims=True)] + [
            jnp.sum(vec[k], axis=0, keepdims=True) for k in range(3)
        ]
        vectors = [row[:, side : side + 128] for row in rows for side in (0, 128)]
        put(320, jnp.concatenate(vectors, axis=0)[None])
        sums_ref[321:] = jnp.zeros((TILES - 321, 8, 128), F32)


def columns(packed, params, earlier):
    def part(which):
        return pl.BlockSpec((MEMBERS, 1, 1, 16, C), lambda p: (0, which, p, 0, 0))

    def whole(shape):
        return pl.BlockSpec(shape, lambda p: (0,) * len(shape))

    pairs = packed.shape[2]
    wide = (HD, 2 * ROWS)
    return pl.pallas_call(
        functools.partial(pair_kernel, pairs, bool(earlier)),
        grid=(pairs,),
        in_specs=[part(0), part(1)] + [whole(a.shape) for a in (*params, *earlier)],
        out_specs=[
            pl.BlockSpec((MEMBERS, 2, 1, 16, C), lambda p: (0, 0, p, 0, 0)),
            whole((TILES, 8, 128)),
        ],
        out_shape=[
            jax.ShapeDtypeStruct(packed.shape, BF16),
            jax.ShapeDtypeStruct((TILES, 8, 128), F32),
        ],
        scratch_shapes=[pltpu.VMEM(wide, BF16)] * 4
        + [
            pltpu.VMEM(wide, F32),
            pltpu.VMEM((4 * HD, 2 * ROWS), BF16),
            pltpu.VMEM((4 * HD, C), F32),
            pltpu.VMEM((HD, C), F32),
            pltpu.VMEM((3, 8, C), F32),
            pltpu.VMEM((HD, 128), F32),
        ],
        compiler_params=pltpu.CompilerParams(
            dimension_semantics=("arbitrary",), vmem_limit_bytes=32 * 2**20
        ),
        cost_estimate=pl.CostEstimate(
            flops=pairs * 4_000_000_000, bytes_accessed=2**23, transcendentals=pairs * 300_000
        ),
    )(packed, packed, *params, *earlier)


def shift(value, axes, size, step):
    return lax.ppermute(value, axes, [(k, (k + step) % size) for k in range(size)])


def scatter_sum(value, axes, size):
    own = lax.axis_index(axes)
    count = value.shape[0] // size

    def block_for(step):
        return lax.dynamic_slice_in_dim(value, lax.rem(own + step, size) * count, count, 0)

    arrived = [shift(block_for(step), axes, size, step) for step in range(1, size)]
    return functools.reduce(jnp.add, arrived, block_for(0))


def gather(value, axes, size):
    own = lax.axis_index(axes)
    count = value.shape[0]
    arrived = [shift(value, axes, size, step) for step in range(1, size)]
    turned = jnp.concatenate(([*reversed(arrived), value]) * 2, axis=0)
    return lax.dynamic_slice_in_dim(turned, (size - 1 - own) * count, size * count, 0)


def all_sum(tiles):
    stages = (("core", 2), ("y", 4), ("x", 4))
    for axes, size in stages:
        tiles = scatter_sum(tiles, axes, size)
    count = tiles.shape[0]
    tiles = jnp.concatenate([tiles, jnp.zeros((16 - count, 8, 128), F32)], axis=0)
    tiles = gather(scatter_sum(tiles, RING, 8) * FACTOR, RING, 8)[:count]
    for axes, size in reversed(stages):
        tiles = gather(tiles, axes, size)
    return tiles


def shards(alignment, cotangent, wq, wk, wv, wg, gate_bias, wo, out_bias, gain, bias):
    structs = alignment.shape[0]
    w = jnp.concatenate([wq, wk, wv, wg], axis=1)
    rows = jnp.concatenate([jnp.stack([out_bias, gain, bias]), jnp.zeros((5, C), F32)], axis=0)
    params = (w, w.T, wo, jnp.broadcast_to(gate_bias[:, None], (HD, 128)), rows)

    def exchange(value):
        return lax.all_to_all(value, DAP, 0, 0, tiled=True)

    arrived = [exchange(pack(alignment, cotangent, s)) for s in range(structs)]
    sums, done = (), ()
    leaving = []
    for s in range(structs):
        results, tiles = columns(arrived[s], params, sums)
        sums = (tiles,)
        leaving.append(exchange(results))
    for s in range(structs):
        done = tuple(unpack(leaving[s], s, structs, done))
    totals = all_sum(sums[0])
    matrices = jnp.concatenate(
        [totals[:160].reshape(5 * HD, 128), totals[160:320].reshape(5 * HD, 128)], axis=1
    ).reshape(5, HD, C)
    vectors = totals[320].reshape(4, C)
    return (*done, matrices[:4], matrices[4], vectors)


def solution(mesh):
    parts = Mesh(mesh.devices.reshape(2, 4, 2, 4, 4), BATCH + DAP)
    split = P(BATCH, DAP, None, None)
    return jax.shard_map(
        shards,
        mesh=parts,
        in_specs=(split, split) + (P(),) * 9,
        out_specs=(split, split, P(), P(), P()),
        check_vma=False,
    )
```

time: 635 us -> 285 us (0.45)
  waiting for transfers between devices: 261 us -> 107 us
  blocking collectives: 143 us -> 0 us
  matrix products: 98.4 us -> 0 us
  starting transfers between devices: 19.7 us -> 86.1 us
  Pallas kernels: 0 us -> 59.6 us
  local copies, waits for them, and re-layouts: 65.7 us -> 24 us
  other arithmetic: 28.3 us -> 6.2 us
  between operations: 14.2 us -> 1.25 us
    psum x1 -> x0, waiting for transfers between devices: 173 us -> none  [shards(): lax.psum((local_sums[0], local_sums[1], local_sums[2]), ('batch', 'dap'))]
    psum x1 -> x0, blocking collectives: 89.2 us -> none  [shards(): lax.psum((local_sums[0], local_sums[1], local_sums[2]), ('batch', 'dap'))]
    dot_general x22 -> x0, matrix products: 83.6 us -> none  [contract(): return jnp.einsum(form, left, right, preferred_element_type=jnp.float32)]
    ppermute x0 -> x28, starting transfers between devices: none -> 59.9 us  [shift(): lax.ppermute(value, axes, [(k, (k + step) % size) for k in range(size)])]
    pallas_call x0 -> x6, Pallas kernels: none -> 59.6 us  [the longest x2 52 us: columns(): pl.pallas_call(functools.partial(pair_kernel, pairs, bool(earlier)), grid...]
    all_to_all x1 -> x0, blocking collectives: 53.9 us -> none  [shards(): lax.all_to_all(new_cols, 'dap', split_axis=1, concat_axis=2, tiled=True)]
    ppermute x0 -> x28, waiting for transfers between devices: none -> 40.5 us  [shift(): lax.ppermute(value, axes, [(k, (k + step) % size) for k in range(size)])]
    all_to_all x3 -> x4, waiting for transfers between devices: 87.9 us -> 66.7 us  [exchange(): return lax.all_to_all(value, DAP, 0, 0, tiled=True)]
  transfers between devices with their start and end apart: 4 -> 32, of which waited for: 3 -> 19; matrix products, arithmetic and copies ran while one was open for 2% -> 3% of each run, Pallas kernels for 0% -> 10%
where the time goes in v1:
time: 285 us; the launch traced here: 284 us
  waiting for transfers between devices  107 us (38%)
  starting transfers between devices  86.1 us (30%)
  Pallas kernels  59.6 us (21%)
  local copies, waits for them, and re-layouts  24 us (8%)
  other arithmetic  6.2 us (2%)
    all_to_all x4, waiting for transfers between devices, exchange(): return lax.all_to_all(value, DAP, 0, 0, tiled=True)  66.7 us
    ppermute x28, starting transfers between devices, shift(): lax.ppermute(value, axes, [(k, (k + step) % size) for k in range(size)])  59.9 us
    pallas_call x2, Pallas kernels, columns(): pl.pallas_call(functools.partial(pair_kernel, pairs, bool(earlier)), grid...  52 us
    ppermute x28, waiting for transfers between devices, shift(): lax.ppermute(value, axes, [(k, (k + step) % size) for k in range(size)])  40.5 us
    all_to_all x4, starting transfers between devices, exchange(): return lax.all_to_all(value, DAP, 0, 0, tiled=True)  26.2 us
    unnamed x93, local copies, waits for them, and re-layouts  21.8 us
  transfers between devices with their start and end apart: 32, of which 19 were waited for; matrix products, arithmetic and copies ran while one was open for 3% of the time, Pallas kernels for 10%

profile of v1, /device:TPU:32, one launch (start us, length us, event | category | flops | bytes accessed | tf_op | source)
XLA Modules:
  0.0 284.4 jit_solution(17007888813089816427)
XLA Ops:
  6.6 8.6 %all-to-all-start.1 = ((bf16[16,2,8,16,256]{4,3,2,1,0:T(8,128)(2,1)}), bf16[16,2,8,16,256]{4,3,2,1,0:T(8,128)(2,1)}, u32[]{:S(2)}, u32[]{:S(2)}) async-start(bf16[16,2,8,16,256]{4,3,2,1,0:T(8,128)(2,1)} %copy-done.5), calls=%async_computation.1 | async-start | bytes 4194304 | tf_op jit(solution)/shard_map/all_to_all | solution.py:305
  19.5 43.0 %all-to-all-done.1.refs_0_.refs_1_ = bf16[16,2,8,16,256]{4,3,2,1,0:T(8,128)(2,1)} async-done(((bf16[16,2,8,16,256]{4,3,2,1,0:T(8,128)(2,1)}), bf16[16,2,8,16,256]{4,3,2,1,0:T(8,128)(2,1)}, u32[]{:S(2)}, u32[]{:S(2)}) %all-to-all-start.1) | async-done | bytes 2097184 | tf_op jit(solution)/shard_map/all_to_all | solution.py:305
  62.6 6.1 %all-to-all-start = ((bf16[16,2,8,16,256]{4,3,2,1,0:T(8,128)(2,1)}), bf16[16,2,8,16,256]{4,3,2,1,0:T(8,128)(2,1)}, u32[]{:S(2)}, u32[]{:S(2)}) async-start(bf16[16,2,8,16,256]{4,3,2,1,0:T(8,128)(2,1)} %copy-done.4), calls=%async_computation | async-start | bytes 4194304 | tf_op jit(solution)/shard_map/all_to_all | solution.py:305
  70.1 26.0 %shard_map.148 = (bf16[16,2,8,16,256]{4,3,2,1,0:T(8,128)(2,1)S(1)}, f32[352,8,128]{2,1,0:T(8,128)S(1)}) custom-call(bf16[16,2,8,16,256]{4,3,2,1,0:T(8,128)(2,1)} %all-to-all-done.1.refs_0_.refs_1_, bf16[16,2,8,16,256]{4,3,2,1,0:T(8,128)(2,1)} %all-to-all-done.1.refs_0_.refs_1_, bf16[256,1024]{1,0:T(8,128)(2,1)S(1)} %copy.23.refs_2_, ...), custom_call_target="tpu_custom_call" | custom-call | flops 32000000000 | bytes 8388608 | tf_op jit(solution)/shard_map/pallas_call | solution.py:233
  99.2 16.0 %all-to-all-done.refs_0_.refs_1_ = bf16[16,2,8,16,256]{4,3,2,1,0:T(8,128)(2,1)} async-done(((bf16[16,2,8,16,256]{4,3,2,1,0:T(8,128)(2,1)}), bf16[16,2,8,16,256]{4,3,2,1,0:T(8,128)(2,1)}, u32[]{:S(2)}, u32[]{:S(2)}) %all-to-all-start) | async-done | bytes 2097184 | tf_op jit(solution)/shard_map/all_to_all | solution.py:305
  120.4 26.0 %shard_map.149 = (bf16[16,2,8,16,256]{4,3,2,1,0:T(8,128)(2,1)S(1)}, f32[352,8,128]{2,1,0:T(8,128)S(1)}) custom-call(bf16[16,2,8,16,256]{4,3,2,1,0:T(8,128)(2,1)} %all-to-all-done.refs_0_.refs_1_, bf16[16,2,8,16,256]{4,3,2,1,0:T(8,128)(2,1)} %all-to-all-done.refs_0_.refs_1_, bf16[256,1024]{1,0:T(8,128)(2,1)S(1)} %copy-done.13, ...), custom_call_target="tpu_custom_call" | custom-call | flops 32000000000 | bytes 8388608 | tf_op jit(solution)/shard_map/pallas_call | solution.py:233
  148.6 6.1 %all-to-all-start.3 = ((bf16[16,2,8,16,256]{4,3,2,1,0:T(8,128)(2,1)}), bf16[16,2,8,16,256]{4,3,2,1,0:T(8,128)(2,1)S(1)}, u32[]{:S(2)}, u32[]{:S(2)}) async-start(bf16[16,2,8,16,256]{4,3,2,1,0:T(8,128)(2,1)} %copy-done.9), calls=%async_computation.3 | async-start | bytes 4194304 | tf_op jit(solution)/shard_map/all_to_all | solution.py:305
  160.2 2.0 collective-permute-start.2
  162.2 2.5 collective-permute-done.1
  164.6 3.2 %collective-permute-done.3 = f32[44,8,128]{2,1,0:T(8,128)S(1)} collective-permute-done((f32[44,8,128]{2,1,0:T(8,128)S(1)}, f32[44,8,128]{2,1,0:T(8,128)S(1)}, u32[]{:S(2)}, u32[]{:S(2)}) %collective-permute-start.3) | collective-permute-done | bytes 180256 | tf_op jit(solution)/shard_map/ppermute | solution.py:264
  181.6 4.5 %collective-permute-start.8 = (f32[2,8,128]{2,1,0:T(8,128)S(1)}, f32[2,8,128]{2,1,0:T(8,128)S(1)}, u32[]{:S(2)}, u32[]{:S(2)}) collective-permute-start(f32[2,8,128]{2,1,0:T(8,128)S(1)} %get-tuple-element.32), channel_id=1, source_target_pairs={{0,8},{4,12},{8,128},{12,132},{128,136},{132,140},{136,0},{140,4},... | collective-permute-start | bytes 24584 | tf_op jit(solution)/shard_map/ppermute | solution.py:264
  186.0 3.4 %collective-permute-start.9 = (f32[2,8,128]{2,1,0:T(8,128)S(1)}, f32[2,8,128]{2,1,0:T(8,128)S(1)}, u32[]{:S(2)}, u32[]{:S(2)}) collective-permute-start(f32[2,8,128]{2,1,0:T(8,128)S(1)} %get-tuple-element.33), channel_id=1, source_target_pairs={{0,12},{4,128},{8,132},{12,136},{128,140},{132,0},{136,4},{140,8},... | collective-permute-start | bytes 24584 | tf_op jit(solution)/shard_map/ppermute | solution.py:264
  190.9 3.1 %collective-permute-start.11 = (f32[2,8,128]{2,1,0:T(8,128)S(1)}, f32[2,8,128]{2,1,0:T(8,128)S(1)}, u32[]{:S(2)}, u32[]{:S(2)}) collective-permute-start(f32[2,8,128]{2,1,0:T(8,128)S(1)} %get-tuple-element.35), channel_id=1, source_target_pairs={{0,132},{4,136},{8,140},{12,0},{128,4},{132,8},{136,12},{140,128},... | collective-permute-start | bytes 24584 | tf_op jit(solution)/shard_map/ppermute | solution.py:264
  194.0 7.7 %collective-permute-done.7 = f32[2,8,128]{2,1,0:T(8,128)S(1)} collective-permute-done((f32[2,8,128]{2,1,0:T(8,128)S(1)}, f32[2,8,128]{2,1,0:T(8,128)S(1)}, u32[]{:S(2)}, u32[]{:S(2)}) %collective-permute-start.7) | collective-permute-done | bytes 8224 | tf_op jit(solution)/shard_map/ppermute | solution.py:264
  201.7 5.9 %collective-permute-start.13 = (f32[2,8,128]{2,1,0:T(8,128)S(1)}, f32[2,8,128]{2,1,0:T(8,128)S(1)}, u32[]{:S(2)}, u32[]{:S(2)}) collective-permute-start(f32[2,8,128]{2,1,0:T(8,128)S(1)} %get-tuple-element.37), channel_id=1, source_target_pairs={{0,140},{4,0},{8,4},{12,8},{128,12},{132,128},{136,132},{140,136},... | collective-permute-start | bytes 24584 | tf_op jit(solution)/shard_map/ppermute | solution.py:264
  209.0 2.4 collective-permute-start.14
  211.3 1.9 collective-permute-start.19
  213.3 3.1 %collective-permute-start.18 = (f32[2,8,128]{2,1,0:T(8,128)S(1)}, f32[2,8,128]{2,1,0:T(8,128)S(1)}, u32[]{:S(2)}, u32[]{:S(2)}) collective-permute-start(f32[2,8,128]{2,1,0:T(8,128)S(1)} %fusion.11), channel_id=1, source_target_pairs={{0,12},{4,128},{8,132},{12,136},{128,140},{132,0},{136,4},{140,8},... | collective-permute-start | bytes 24584 | tf_op jit(solution)/shard_map/ppermute | solution.py:264
  217.9 4.1 %collective-permute-start.15 = (f32[2,8,128]{2,1,0:T(8,128)S(1)}, f32[2,8,128]{2,1,0:T(8,128)S(1)}, u32[]{:S(2)}, u32[]{:S(2)}) collective-permute-start(f32[2,8,128]{2,1,0:T(8,128)S(1)} %fusion.11), channel_id=1, source_target_pairs={{0,136},{4,140},{8,0},{12,4},{128,8},{132,12},{136,128},{140,132},... | collective-permute-start | bytes 24584 | tf_op jit(solution)/shard_map/ppermute | solution.py:264
  223.3 5.1 %collective-permute-start.16 = (f32[2,8,128]{2,1,0:T(8,128)S(1)}, f32[2,8,128]{2,1,0:T(8,128)S(1)}, u32[]{:S(2)}, u32[]{:S(2)}) collective-permute-start(f32[2,8,128]{2,1,0:T(8,128)S(1)} %fusion.11), channel_id=1, source_target_pairs={{0,132},{4,136},{8,140},{12,0},{128,4},{132,8},{136,12},{140,128},... | collective-permute-start | bytes 24584 | tf_op jit(solution)/shard_map/ppermute | solution.py:264
  230.2 3.1 %collective-permute-start.21 = (f32[11,8,128]{2,1,0:T(8,128)S(1)}, f32[11,8,128]{2,1,0:T(8,128)S(1)}, u32[]{:S(2)}, u32[]{:S(2)}) collective-permute-start(f32[11,8,128]{2,1,0:T(8,128)S(1)} %constant_dynamic-slice_fusion.2), channel_id=1, source_target_pairs={{0,3},{1,0},{2,1},{3,2},{4,7},{5,4},{6,5},{7,6},{8,11},{9,8},{10,9... | collective-permute-start | bytes 135176 | tf_op jit(solution)/shard_map/ppermute | solution.py:264
  234.6 5.3 %all-to-all-start.2 = ((bf16[16,2,8,16,256]{4,3,2,1,0:T(8,128)(2,1)}), bf16[16,2,8,16,256]{4,3,2,1,0:T(8,128)(2,1)S(1)}, u32[]{:S(2)}, u32[]{:S(2)}) async-start(bf16[16,2,8,16,256]{4,3,2,1,0:T(8,128)(2,1)} %copy-done.8), calls=%async_computation.2 | async-start | bytes 4194304 | tf_op jit(solution)/shard_map/all_to_all | solution.py:305
  241.4 2.7 collective-permute-start.22
  244.1 7.8 %collective-permute-done.22 = f32[11,8,128]{2,1,0:T(8,128)S(1)} collective-permute-done((f32[11,8,128]{2,1,0:T(8,128)S(1)}, f32[11,8,128]{2,1,0:T(8,128)S(1)}, u32[]{:S(2)}, u32[]{:S(2)}) %collective-permute-start.22) | collective-permute-done | bytes 45088 | tf_op jit(solution)/shard_map/ppermute | solution.py:264
  252.0 2.8 collective-permute-start.24
  256.6 3.3 %collective-permute-done.24 = f32[44,8,128]{2,1,0:T(8,128)S(1)} collective-permute-done((f32[44,8,128]{2,1,0:T(8,128)S(1)}, f32[44,8,128]{2,1,0:T(8,128)S(1)}, u32[]{:S(2)}, u32[]{:S(2)}) %collective-permute-start.24) | collective-permute-done | bytes 180256 | tf_op jit(solution)/shard_map/ppermute | solution.py:264
  259.8 2.1 collective-permute-done.25
  262.0 1.8 collective-permute-done.26
  266.4 2.1 fusion.2
  271.9 2.4 shard_map.150
  274.3 7.7 %all-to-all-done.2.refs_0_ = bf16[16,2,8,16,256]{4,3,2,1,0:T(8,128)(2,1)S(1)} async-done(((bf16[16,2,8,16,256]{4,3,2,1,0:T(8,128)(2,1)}), bf16[16,2,8,16,256]{4,3,2,1,0:T(8,128)(2,1)S(1)}, u32[]{:S(2)}, u32[]{:S(2)}) %all-to-all-start.2) | async-done | bytes 2097184 | tf_op jit(solution)/shard_map/all_to_all | solution.py:305
  282.0 2.4 shard_map.151
  (157 shorter events, 59.1 us)
Async XLA Ops:
  6.6 56.0 %all-to-all-start.1 = ((bf16[16,2,8,16,256]{4,3,2,1,0:T(8,128)(2,1)}), bf16[16,2,8,16,256]{4,3,2,1,0:T(8,128)(2,1)}, u32[]{:S(2)}, u32[]{:S(2)}) async-start(bf16[16,2,8,16,256]{4,3,2,1,0:T(8,128)(2,1)} %copy-done.5), calls=%async_computation.1 | async-start | bytes 4194304 | tf_op jit(solution)/shard_map/all_to_all | solution.py:305
  62.6 52.6 %all-to-all-start = ((bf16[16,2,8,16,256]{4,3,2,1,0:T(8,128)(2,1)}), bf16[16,2,8,16,256]{4,3,2,1,0:T(8,128)(2,1)}, u32[]{:S(2)}, u32[]{:S(2)}) async-start(bf16[16,2,8,16,256]{4,3,2,1,0:T(8,128)(2,1)} %copy-done.4), calls=%async_computation | async-start | bytes 4194304 | tf_op jit(solution)/shard_map/all_to_all | solution.py:305
  148.6 6.1 %collective-permute-start = (f32[176,8,128]{2,1,0:T(8,128)}, f32[176,8,128]{2,1,0:T(8,128)}, u32[]{:S(2)}, u32[]{:S(2)}) collective-permute-start(f32[176,8,128]{2,1,0:T(8,128)} %constant_dynamic-slice_fusion.9), channel_id=1, source_target_pairs={{0,16},{16,0},{1,17},{17,1},{2,18},{18,2},{3,19},{19,3},{4,20},{20... | collective-permute-start | bytes 2162696 | tf_op jit(solution)/shard_map/ppermute | solution.py:264
  148.6 84.7 %all-to-all-start.3 = ((bf16[16,2,8,16,256]{4,3,2,1,0:T(8,128)(2,1)}), bf16[16,2,8,16,256]{4,3,2,1,0:T(8,128)(2,1)S(1)}, u32[]{:S(2)}, u32[]{:S(2)}) async-start(bf16[16,2,8,16,256]{4,3,2,1,0:T(8,128)(2,1)} %copy-done.9), calls=%async_computation.3 | async-start | bytes 4194304 | tf_op jit(solution)/shard_map/all_to_all | solution.py:305
  156.9 7.8 %collective-permute-start.1 = (f32[44,8,128]{2,1,0:T(8,128)S(1)}, f32[44,8,128]{2,1,0:T(8,128)S(1)}, u32[]{:S(2)}, u32[]{:S(2)}) collective-permute-start(f32[44,8,128]{2,1,0:T(8,128)S(1)} %get-tuple-element.23), channel_id=1, source_target_pairs={{0,32},{32,64},{64,96},{96,0},{1,33},{33,65},{65,97},{97,1},{2,34}... | collective-permute-start | bytes 540680 | tf_op jit(solution)/shard_map/ppermute | solution.py:264
  158.5 9.3 %collective-permute-start.3 = (f32[44,8,128]{2,1,0:T(8,128)S(1)}, f32[44,8,128]{2,1,0:T(8,128)S(1)}, u32[]{:S(2)}, u32[]{:S(2)}) collective-permute-start(f32[44,8,128]{2,1,0:T(8,128)S(1)} %get-tuple-element.24), channel_id=1, source_target_pairs={{0,96},{32,0},{64,32},{96,64},{1,97},{33,1},{65,33},{97,65},{2,98}... | collective-permute-start | bytes 540680 | tf_op jit(solution)/shard_map/ppermute | solution.py:264
  160.2 9.5 %collective-permute-start.2 = (f32[44,8,128]{2,1,0:T(8,128)S(1)}, f32[44,8,128]{2,1,0:T(8,128)S(1)}, u32[]{:S(2)}, u32[]{:S(2)}) collective-permute-start(f32[44,8,128]{2,1,0:T(8,128)S(1)} %get-tuple-element.25), channel_id=1, source_target_pairs={{0,64},{32,96},{64,0},{96,32},{1,65},{33,97},{65,1},{97,33},{2,66}... | collective-permute-start | bytes 540680 | tf_op jit(solution)/shard_map/ppermute | solution.py:264
  170.6 6.7 %collective-permute-start.4 = (f32[11,8,128]{2,1,0:T(8,128)S(1)}, f32[11,8,128]{2,1,0:T(8,128)S(1)}, u32[]{:S(2)}, u32[]{:S(2)}) collective-permute-start(f32[11,8,128]{2,1,0:T(8,128)S(1)} %get-tuple-element.28), channel_id=1, source_target_pairs={{0,1},{1,2},{2,3},{3,0},{4,5},{5,6},{6,7},{7,4},{8,9},{9,10},{10,1... | collective-permute-start | bytes 135176 | tf_op jit(solution)/shard_map/ppermute | solution.py:264
  172.2 6.8 %collective-permute-start.6 = (f32[11,8,128]{2,1,0:T(8,128)S(1)}, f32[11,8,128]{2,1,0:T(8,128)S(1)}, u32[]{:S(2)}, u32[]{:S(2)}) collective-permute-start(f32[11,8,128]{2,1,0:T(8,128)S(1)} %get-tuple-element.29), channel_id=1, source_target_pairs={{0,3},{1,0},{2,1},{3,2},{4,7},{5,4},{6,5},{7,6},{8,11},{9,8},{10,9... | collective-permute-start | bytes 135176 | tf_op jit(solution)/shard_map/ppermute | solution.py:264
  174.0 6.2 %collective-permute-start.5 = (f32[11,8,128]{2,1,0:T(8,128)S(1)}, f32[11,8,128]{2,1,0:T(8,128)S(1)}, u32[]{:S(2)}, u32[]{:S(2)}) collective-permute-start(f32[11,8,128]{2,1,0:T(8,128)S(1)} %get-tuple-element.30), channel_id=1, source_target_pairs={{0,2},{1,3},{2,0},{3,1},{4,6},{5,7},{6,4},{7,5},{8,10},{9,11},{10,... | collective-permute-start | bytes 135176 | tf_op jit(solution)/shard_map/ppermute | solution.py:264
  180.3 21.4 %collective-permute-start.7 = (f32[2,8,128]{2,1,0:T(8,128)S(1)}, f32[2,8,128]{2,1,0:T(8,128)S(1)}, u32[]{:S(2)}, u32[]{:S(2)}) collective-permute-start(f32[2,8,128]{2,1,0:T(8,128)S(1)} %get-tuple-element.31), channel_id=1, source_target_pairs={{0,4},{4,8},{8,12},{12,128},{128,132},{132,136},{136,140},{140,0},... | collective-permute-start | bytes 24584 | tf_op jit(solution)/shard_map/ppermute | solution.py:264
  181.6 20.1 %collective-permute-start.8 = (f32[2,8,128]{2,1,0:T(8,128)S(1)}, f32[2,8,128]{2,1,0:T(8,128)S(1)}, u32[]{:S(2)}, u32[]{:S(2)}) collective-permute-start(f32[2,8,128]{2,1,0:T(8,128)S(1)} %get-tuple-element.32), channel_id=1, source_target_pairs={{0,8},{4,12},{8,128},{12,132},{128,136},{132,140},{136,0},{140,4},... | collective-permute-start | bytes 24584 | tf_op jit(solution)/shard_map/ppermute | solution.py:264
  186.0 21.6 %collective-permute-start.9 = (f32[2,8,128]{2,1,0:T(8,128)S(1)}, f32[2,8,128]{2,1,0:T(8,128)S(1)}, u32[]{:S(2)}, u32[]{:S(2)}) collective-permute-start(f32[2,8,128]{2,1,0:T(8,128)S(1)} %get-tuple-element.33), channel_id=1, source_target_pairs={{0,12},{4,128},{8,132},{12,136},{128,140},{132,0},{136,4},{140,8},... | collective-permute-start | bytes 24584 | tf_op jit(solution)/shard_map/ppermute | solution.py:264
  189.4 18.2 %collective-permute-start.10 = (f32[2,8,128]{2,1,0:T(8,128)S(1)}, f32[2,8,128]{2,1,0:T(8,128)S(1)}, u32[]{:S(2)}, u32[]{:S(2)}) collective-permute-start(f32[2,8,128]{2,1,0:T(8,128)S(1)} %get-tuple-element.34), channel_id=1, source_target_pairs={{0,128},{4,132},{8,136},{12,140},{128,0},{132,4},{136,8},{140,12},... | collective-permute-start | bytes 24584 | tf_op jit(solution)/shard_map/ppermute | solution.py:264
  190.9 16.7 %collective-permute-start.11 = (f32[2,8,128]{2,1,0:T(8,128)S(1)}, f32[2,8,128]{2,1,0:T(8,128)S(1)}, u32[]{:S(2)}, u32[]{:S(2)}) collective-permute-start(f32[2,8,128]{2,1,0:T(8,128)S(1)} %get-tuple-element.35), channel_id=1, source_target_pairs={{0,132},{4,136},{8,140},{12,0},{128,4},{132,8},{136,12},{140,128},... | collective-permute-start | bytes 24584 | tf_op jit(solution)/shard_map/ppermute | solution.py:264
  201.6 6.0 %collective-permute-start.12 = (f32[2,8,128]{2,1,0:T(8,128)S(1)}, f32[2,8,128]{2,1,0:T(8,128)S(1)}, u32[]{:S(2)}, u32[]{:S(2)}) collective-permute-start(f32[2,8,128]{2,1,0:T(8,128)S(1)} %get-tuple-element.36), channel_id=1, source_target_pairs={{0,136},{4,140},{8,0},{12,4},{128,8},{132,12},{136,128},{140,132},... | collective-permute-start | bytes 24584 | tf_op jit(solution)/shard_map/ppermute | solution.py:264
  201.7 7.3 %collective-permute-start.13 = (f32[2,8,128]{2,1,0:T(8,128)S(1)}, f32[2,8,128]{2,1,0:T(8,128)S(1)}, u32[]{:S(2)}, u32[]{:S(2)}) collective-permute-start(f32[2,8,128]{2,1,0:T(8,128)S(1)} %get-tuple-element.37), channel_id=1, source_target_pairs={{0,140},{4,0},{8,4},{12,8},{128,12},{132,128},{136,132},{140,136},... | collective-permute-start | bytes 24584 | tf_op jit(solution)/shard_map/ppermute | solution.py:264
  209.0 8.9 %collective-permute-start.14 = (f32[2,8,128]{2,1,0:T(8,128)S(1)}, f32[2,8,128]{2,1,0:T(8,128)S(1)}, u32[]{:S(2)}, u32[]{:S(2)}) collective-permute-start(f32[2,8,128]{2,1,0:T(8,128)S(1)} %fusion.11), channel_id=1, source_target_pairs={{0,140},{4,0},{8,4},{12,8},{128,12},{132,128},{136,132},{140,136},... | collective-permute-start | bytes 24584 | tf_op jit(solution)/shard_map/ppermute | solution.py:264
  211.3 18.7 %collective-permute-start.20 = (f32[2,8,128]{2,1,0:T(8,128)S(1)}, f32[2,8,128]{2,1,0:T(8,128)S(1)}, u32[]{:S(2)}, u32[]{:S(2)}) collective-permute-start(f32[2,8,128]{2,1,0:T(8,128)S(1)} %fusion.11), channel_id=1, source_target_pairs={{0,4},{4,8},{8,12},{12,128},{128,132},{132,136},{136,140},{140,0},... | collective-permute-start | bytes 24584 | tf_op jit(solution)/shard_map/ppermute | solution.py:264
  211.3 18.7 %collective-permute-start.19 = (f32[2,8,128]{2,1,0:T(8,128)S(1)}, f32[2,8,128]{2,1,0:T(8,128)S(1)}, u32[]{:S(2)}, u32[]{:S(2)}) collective-permute-start(f32[2,8,128]{2,1,0:T(8,128)S(1)} %fusion.11), channel_id=1, source_target_pairs={{0,8},{4,12},{8,128},{12,132},{128,136},{132,140},{136,0},{140,4},... | collective-permute-start | bytes 24584 | tf_op jit(solution)/shard_map/ppermute | solution.py:264
  213.3 16.7 %collective-permute-start.18 = (f32[2,8,128]{2,1,0:T(8,128)S(1)}, f32[2,8,128]{2,1,0:T(8,128)S(1)}, u32[]{:S(2)}, u32[]{:S(2)}) collective-permute-start(f32[2,8,128]{2,1,0:T(8,128)S(1)} %fusion.11), channel_id=1, source_target_pairs={{0,12},{4,128},{8,132},{12,136},{128,140},{132,0},{136,4},{140,8},... | collective-permute-start | bytes 24584 | tf_op jit(solution)/shard_map/ppermute | solution.py:264
  216.4 13.6 %collective-permute-start.17 = (f32[2,8,128]{2,1,0:T(8,128)S(1)}, f32[2,8,128]{2,1,0:T(8,128)S(1)}, u32[]{:S(2)}, u32[]{:S(2)}) collective-permute-start(f32[2,8,128]{2,1,0:T(8,128)S(1)} %fusion.11), channel_id=1, source_target_pairs={{0,128},{4,132},{8,136},{12,140},{128,0},{132,4},{136,8},{140,12},... | collective-permute-start | bytes 24584 | tf_op jit(solution)/shard_map/ppermute | solution.py:264
  217.9 5.4 %collective-permute-start.15 = (f32[2,8,128]{2,1,0:T(8,128)S(1)}, f32[2,8,128]{2,1,0:T(8,128)S(1)}, u32[]{:S(2)}, u32[]{:S(2)}) collective-permute-start(f32[2,8,128]{2,1,0:T(8,128)S(1)} %fusion.11), channel_id=1, source_target_pairs={{0,136},{4,140},{8,0},{12,4},{128,8},{132,12},{136,128},{140,132},... | collective-permute-start | bytes 24584 | tf_op jit(solution)/shard_map/ppermute | solution.py:264
  223.3 6.7 %collective-permute-start.16 = (f32[2,8,128]{2,1,0:T(8,128)S(1)}, f32[2,8,128]{2,1,0:T(8,128)S(1)}, u32[]{:S(2)}, u32[]{:S(2)}) collective-permute-start(f32[2,8,128]{2,1,0:T(8,128)S(1)} %fusion.11), channel_id=1, source_target_pairs={{0,132},{4,136},{8,140},{12,0},{128,4},{132,8},{136,12},{140,128},... | collective-permute-start | bytes 24584 | tf_op jit(solution)/shard_map/ppermute | solution.py:264
  230.2 13.9 %collective-permute-start.21 = (f32[11,8,128]{2,1,0:T(8,128)S(1)}, f32[11,8,128]{2,1,0:T(8,128)S(1)}, u32[]{:S(2)}, u32[]{:S(2)}) collective-permute-start(f32[11,8,128]{2,1,0:T(8,128)S(1)} %constant_dynamic-slice_fusion.2), channel_id=1, source_target_pairs={{0,3},{1,0},{2,1},{3,2},{4,7},{5,4},{6,5},{7,6},{8,11},{9,8},{10,9... | collective-permute-start | bytes 135176 | tf_op jit(solution)/shard_map/ppermute | solution.py:264
  234.6 47.4 %all-to-all-start.2 = ((bf16[16,2,8,16,256]{4,3,2,1,0:T(8,128)(2,1)}), bf16[16,2,8,16,256]{4,3,2,1,0:T(8,128)(2,1)S(1)}, u32[]{:S(2)}, u32[]{:S(2)}) async-start(bf16[16,2,8,16,256]{4,3,2,1,0:T(8,128)(2,1)} %copy-done.8), calls=%async_computation.2 | async-start | bytes 4194304 | tf_op jit(solution)/shard_map/all_to_all | solution.py:305
  239.9 12.0 %collective-permute-start.23 = (f32[11,8,128]{2,1,0:T(8,128)S(1)}, f32[11,8,128]{2,1,0:T(8,128)S(1)}, u32[]{:S(2)}, u32[]{:S(2)}) collective-permute-start(f32[11,8,128]{2,1,0:T(8,128)S(1)} %constant_dynamic-slice_fusion.2), channel_id=1, source_target_pairs={{0,1},{1,2},{2,3},{3,0},{4,5},{5,6},{6,7},{7,4},{8,9},{9,10},{10,1... | collective-permute-start | bytes 135176 | tf_op jit(solution)/shard_map/ppermute | solution.py:264
  241.4 10.5 %collective-permute-start.22 = (f32[11,8,128]{2,1,0:T(8,128)S(1)}, f32[11,8,128]{2,1,0:T(8,128)S(1)}, u32[]{:S(2)}, u32[]{:S(2)}) collective-permute-start(f32[11,8,128]{2,1,0:T(8,128)S(1)} %constant_dynamic-slice_fusion.2), channel_id=1, source_target_pairs={{0,2},{1,3},{2,0},{3,1},{4,6},{5,7},{6,4},{7,5},{8,10},{9,11},{10,... | collective-permute-start | bytes 135176 | tf_op jit(solution)/shard_map/ppermute | solution.py:264
  252.0 7.8 %collective-permute-start.24 = (f32[44,8,128]{2,1,0:T(8,128)S(1)}, f32[44,8,128]{2,1,0:T(8,128)S(1)}, u32[]{:S(2)}, u32[]{:S(2)}) collective-permute-start(f32[44,8,128]{2,1,0:T(8,128)S(1)} %constant_dynamic-slice_fusion.1), channel_id=1, source_target_pairs={{0,96},{32,0},{64,32},{96,64},{1,97},{33,1},{65,33},{97,65},{2,98}... | collective-permute-start | bytes 540680 | tf_op jit(solution)/shard_map/ppermute | solution.py:264
  254.9 7.1 %collective-permute-start.25 = (f32[44,8,128]{2,1,0:T(8,128)S(1)}, f32[44,8,128]{2,1,0:T(8,128)S(1)}, u32[]{:S(2)}, u32[]{:S(2)}) collective-permute-start(f32[44,8,128]{2,1,0:T(8,128)S(1)} %constant_dynamic-slice_fusion.1), channel_id=1, source_target_pairs={{0,64},{32,96},{64,0},{96,32},{1,65},{33,97},{65,1},{97,33},{2,66}... | collective-permute-start | bytes 540680 | tf_op jit(solution)/shard_map/ppermute | solution.py:264
  255.8 8.0 %collective-permute-start.26 = (f32[44,8,128]{2,1,0:T(8,128)S(1)}, f32[44,8,128]{2,1,0:T(8,128)S(1)}, u32[]{:S(2)}, u32[]{:S(2)}) collective-permute-start(f32[44,8,128]{2,1,0:T(8,128)S(1)} %constant_dynamic-slice_fusion.1), channel_id=1, source_target_pairs={{0,32},{32,64},{64,96},{96,0},{1,33},{33,65},{65,97},{97,1},{2,34}... | collective-permute-start | bytes 540680 | tf_op jit(solution)/shard_map/ppermute | solution.py:264
  264.0 2.4 collective-permute-start.27
  (30 other events, 285.1 us)

commit v2 on v1

--- a/solution.py
+++ b/solution.py
@@ -24,13 +24,15 @@
 
 MEMBERS = 16
 OWN_ROWS = ROWS // MEMBERS
-OWN_RES = RES // MEMBERS
-PAIRS = OWN_RES // 2
+QUADS = 2
+PAIRS = 4
+HALF_RES = RES // QUADS
 DAP = ("z_lo", "x")
 BATCH = ("z_hi", "y", "core")
-RING = ("z_hi", "z_lo")
 TILES = 352
-GROUP = 4
+GROUP = 8
+COUNT = GROUP * 2 * PAIRS
+VMEM = 60 * 2**20
 
 
 def dot(left, right, left_dim=1, right_dim=0):
@@ -39,61 +41,64 @@
     )
 
 
+def quad_specs(first):
+    rows = pl.BlockSpec(
+        (1, OWN_ROWS, COUNT, C),
+        lambda n, g: ((first + n) // QUADS, 0, (first + n) % QUADS * (MEMBERS // GROUP) + g, 0),
+    )
+    packed = pl.BlockSpec((GROUP, 2, PAIRS, 16, C), lambda n, g: (g, 0, n, 0, 0))
+    return rows, packed
+
+
 def pack_kernel(x_ref, cot_ref, out_ref, wide):
-    count = GROUP * OWN_RES
     for which, ref in enumerate((x_ref, cot_ref)):
-        for row in range(OWN_ROWS):
-            for side in range(2):
-                wide[side, pl.ds(row, count, stride=OWN_ROWS), :] = ref[
-                    0, row, :, side * 128 : side * 128 + 128
-                ].astype(F32)
         for side in range(2):
-            out_ref[:, which, :, :, side * 128 : side * 128 + 128] = (
-                wide[side].reshape(GROUP, PAIRS, 16, 128).astype(BF16)
-            )
-
-
-def pack(alignment, cotangent, struct):
-    block = pl.BlockSpec((1, OWN_ROWS, GROUP * OWN_RES, C), lambda g: (struct, 0, g, 0))
+            lanes = slice(side * 128, side * 128 + 128)
+            for row in range(OWN_ROWS):
+                wide[which, side, pl.ds(row, COUNT, stride=OWN_ROWS), :] = ref[0, row, :, lanes].astype(F32)
+            out_ref[:, which, :, :, lanes] = wide[which, side].reshape(GROUP, PAIRS, 16, 128).astype(BF16)
+
+
+def pack(alignment, cotangent, first, quads):
+    rows, packed = quad_specs(first)
     return pl.pallas_call(
         pack_kernel,
-        grid=(MEMBERS // GROUP,),
-        in_specs=[block, block],
-        out_specs=pl.BlockSpec((GROUP, 2, PAIRS, 16, C), lambda g: (g, 0, 0, 0, 0)),
-        out_shape=jax.ShapeDtypeStruct((MEMBERS, 2, PAIRS, 16, C), BF16),
-        scratch_shapes=[pltpu.VMEM((2, GROUP * OWN_RES * OWN_ROWS, 128), F32)],
-        compiler_params=pltpu.CompilerParams(vmem_limit_bytes=16 * 2**20),
-        cost_estimate=pl.CostEstimate(flops=0, bytes_accessed=2**22, transcendentals=0),
+        grid=(quads, MEMBERS // GROUP),
+        in_specs=[rows, rows],
+        out_specs=packed,
+        out_shape=pltpu.HBM((MEMBERS, 2, quads * PAIRS, 16, C), BF16),
+        scratch_shapes=[pltpu.VMEM((2, 2, COUNT * OWN_ROWS, 128), F32)],
+        compiler_params=pltpu.CompilerParams(vmem_limit_bytes=VMEM),
+        cost_estimate=pl.CostEstimate(flops=0, bytes_accessed=quads * 2**21, transcendentals=0),
     )(alignment, cotangent)
 
 
 def unpack_kernel(*refs):
     in_ref, upd_ref, grad_ref, wide = refs[0], *refs[-3:]
-    count = GROUP * OWN_RES
     for which, ref in enumerate((upd_ref, grad_ref)):
         for side in range(2):
             lanes = slice(side * 128, side * 128 + 128)
-            wide[side] = in_ref[:, which, :, :, lanes].astype(F32).reshape(count * OWN_ROWS, 128)
+            wide[which, side] = in_ref[:, which, :, :, lanes].astype(F32).reshape(COUNT * OWN_ROWS, 128)
             for row in range(OWN_ROWS):
                 ref[0, row, :, lanes] = wide[
-                    side, pl.ds(row, count, stride=OWN_ROWS), :
+                    which, side, pl.ds(row, COUNT, stride=OWN_ROWS), :
                 ].astype(BF16)
 
 
-def unpack(packed, struct, structs, earlier):
-    block = pl.BlockSpec((1, OWN_ROWS, GROUP * OWN_RES, C), lambda g: (struct, 0, g, 0))
-    shape = jax.ShapeDtypeStruct((structs, OWN_ROWS, RES, C), BF16)
+def unpack(packed, first, structs, earlier):
+    rows, blocks = quad_specs(first)
+    shape = pltpu.HBM((structs, OWN_ROWS, RES, C), BF16)
+    quads = packed.shape[2] // PAIRS
     return pl.pallas_call(
         unpack_kernel,
-        grid=(MEMBERS // GROUP,),
-        in_specs=[pl.BlockSpec((GROUP, 2, PAIRS, 16, C), lambda g: (g, 0, 0, 0, 0))]
-        + [pl.BlockSpec(memory_space=pl.ANY)] * len(earlier),
-        out_specs=[block, block],
+        grid=(quads, MEMBERS // GROUP),
+        in_specs=[blocks] + [pl.BlockSpec(memory_space=pl.ANY)] * len(earlier),
+        out_specs=[rows, rows],
         out_shape=[shape, shape],
         input_output_aliases={1 + k: k for k in range(len(earlier))},
-        scratch_shapes=[pltpu.VMEM((2, GROUP * OWN_RES * OWN_ROWS, 128), F32)],
-        compiler_params=pltpu.CompilerParams(vmem_limit_bytes=16 * 2**20),
-        cost_estimate=pl.CostEstimate(flops=0, bytes_accessed=2**22, transcendentals=0),
+        scratch_shapes=[pltpu.VMEM((2, 2, COUNT * OWN_ROWS, 128), F32)],
+        compiler_params=pltpu.CompilerParams(vmem_limit_bytes=24 * 2**20),
+        cost_estimate=pl.CostEstimate(flops=0, bytes_accessed=quads * 2**21, transcendentals=0),
     )(packed, *earlier)
 
 
@@ -117,9 +122,10 @@
     return matrix[:, :128].reshape(count, 8, 128), matrix[:, 128:].reshape(count, 8, 128)
 
 
-def pair_kernel(steps, has_earlier, *refs):
+def pair_kernel(steps, early, has_earlier, *refs):
     x_ref, cot_ref, w_ref, wt_ref, wo_ref, gb_ref, rows_ref = refs[:7]
-    out_ref, sums_ref, qc, kc, vc, dac, attc, dprojc, gin, gout, vec, dlog = refs[-12:]
+    early_ref = refs[-13]
+    late_ref, sums_ref, qc, kc, vc, dac, attc, dprojc, gin, gout, vec, dlog = refs[-12:]
 
     @pl.when(pl.program_id(0) == 0)
     def _():
@@ -186,7 +192,7 @@
     gin[...] += dot(dprojc[...], normed)
     gout[...] += dot(gated_half, cot_half)
     update = dot(gated_half.T, wo_ref[...]) + out_bias
-    out_ref[:, 0, 0] = row_blocks(x + update).astype(BF16)
+    updated = row_blocks(x + update).astype(BF16)
     d_normed = dot(w_ref[...], dprojc[...]).T
     d_hat = d_normed * gain
     d_std = d_normed * standard
@@ -195,7 +201,17 @@
         - jnp.mean(d_hat, axis=-1, keepdims=True)
         - standard * jnp.mean(d_hat * standard, axis=-1, keepdims=True)
     )
-    out_ref[:, 1, 0] = row_blocks(cot + branch).astype(BF16)
+    grad = row_blocks(cot + branch).astype(BF16)
+
+    def store(ref):
+        ref[:, 0, 0] = updated
+        ref[:, 1, 0] = grad
+
+    if early:
+        pl.when(pl.program_id(0) < early)(lambda: store(early_ref))
+        pl.when(pl.program_id(0) >= early)(lambda: store(late_ref))
+    else:
+        store(late_ref)
     vec[0] += fold_rows(cot)
     vec[1] += fold_rows(d_std)
     vec[2] += fold_rows(d_normed)
@@ -221,7 +237,7 @@
         sums_ref[321:] = jnp.zeros((TILES - 321, 8, 128), F32)
 
 
-def columns(packed, params, earlier):
+def columns(packed, params, early, late, sums=None, filled=None):
     def part(which):
         return pl.BlockSpec((MEMBERS, 1, 1, 16, C), lambda p: (0, which, p, 0, 0))
 
@@ -229,19 +245,31 @@
         return pl.BlockSpec(shape, lambda p: (0,) * len(shape))
 
     pairs = packed.shape[2]
+    later = (sums, filled) if filled is not None else ()
+    offset = late - pairs if later else -early
+    out_block = (MEMBERS, 2, 1, 16, C)
+    out_specs = [
+        pl.BlockSpec(out_block, lambda p: (0, 0, jnp.maximum(p + offset, 0), 0, 0)),
+        whole((TILES, 8, 128)),
+    ]
+    out_shape = [
+        pltpu.HBM((MEMBERS, 2, late, 16, C), BF16),
+        jax.ShapeDtypeStruct((TILES, 8, 128), F32),
+    ]
+    if early:
+        out_specs.insert(0, pl.BlockSpec(out_block, lambda p: (0, 0, jnp.minimum(p, early - 1), 0, 0)))
+        out_shape.insert(0, pltpu.HBM((MEMBERS, 2, early, 16, C), BF16))
+    in_specs = [part(0), part(1)] + [whole(a.shape) for a in params]
+    if later:
+        in_specs += [whole(sums.shape), pl.BlockSpec(memory_space=pl.ANY)]
     wide = (HD, 2 * ROWS)
     return pl.pallas_call(
-        functools.partial(pair_kernel, pairs, bool(earlier)),
+        functools.partial(pair_kernel, pairs, early, bool(later)),
         grid=(pairs,),
-        in_specs=[part(0), part(1)] + [whole(a.shape) for a in (*params, *earlier)],
-        out_specs=[
-            pl.BlockSpec((MEMBERS, 2, 1, 16, C), lambda p: (0, 0, p, 0, 0)),
-            whole((TILES, 8, 128)),
-        ],
-        out_shape=[
-            jax.ShapeDtypeStruct(packed.shape, BF16),
-            jax.ShapeDtypeStruct((TILES, 8, 128), F32),
-        ],
+        in_specs=in_specs,
+        out_specs=out_specs,
+        out_shape=out_shape,
+        input_output_aliases={len(in_specs) - 1: 0} if later else {},
         scratch_shapes=[pltpu.VMEM(wide, BF16)] * 4
         + [
             pltpu.VMEM(wide, F32),
@@ -257,7 +285,7 @@
         cost_estimate=pl.CostEstimate(
             flops=pairs * 4_000_000_000, bytes_accessed=2**23, transcendentals=pairs * 300_000
         ),
-    )(packed, packed, *params, *earlier)
+    )(packed, packed, *params, *later)
 
 
 def shift(value, axes, size, step):
@@ -279,17 +307,24 @@
     own = lax.axis_index(axes)
     count = value.shape[0]
     arrived = [shift(value, axes, size, step) for step in range(1, size)]
-    turned = jnp.concatenate(([*reversed(arrived), value]) * 2, axis=0)
-    return lax.dynamic_slice_in_dim(turned, (size - 1 - own) * count, size * count, 0)
+    total = jnp.zeros((size * count, *value.shape[1:]), value.dtype)
+    for step, piece in enumerate([value, *arrived]):
+        place = lax.rem(own + size - step, size) * count
+        total = lax.dynamic_update_slice_in_dim(total, piece, place, 0)
+    return total
+
+
+def swap_sum(value, axis, size, bit):
+    return value + lax.ppermute(value, axis, [(k, k ^ bit) for k in range(size)])
 
 
 def all_sum(tiles):
     stages = (("core", 2), ("y", 4), ("x", 4))
     for axes, size in stages:
         tiles = scatter_sum(tiles, axes, size)
-    count = tiles.shape[0]
-    tiles = jnp.concatenate([tiles, jnp.zeros((16 - count, 8, 128), F32)], axis=0)
-    tiles = gather(scatter_sum(tiles, RING, 8) * FACTOR, RING, 8)[:count]
+    tiles = swap_sum(tiles, "z_lo", 4, 1)
+    tiles = swap_sum(tiles, "z_lo", 4, 2)
+    tiles = swap_sum(tiles, "z_hi", 2, 1) * FACTOR
     for axes, size in reversed(stages):
         tiles = gather(tiles, axes, size)
     return tiles
@@ -304,16 +339,15 @@
     def exchange(value):
         return lax.all_to_all(value, DAP, 0, 0, tiled=True)
 
-    arrived = [exchange(pack(alignment, cotangent, s)) for s in range(structs)]
-    sums, done = (), ()
-    leaving = []
-    for s in range(structs):
-        results, tiles = columns(arrived[s], params, sums)
-        sums = (tiles,)
-        leaving.append(exchange(results))
-    for s in range(structs):
-        done = tuple(unpack(leaving[s], s, structs, done))
-    totals = all_sum(sums[0])
+    first = exchange(pack(alignment, cotangent, 0, 2))
+    second = exchange(pack(alignment, cotangent, 2, 2))
+    early, late, sums = columns(first, params, PAIRS, 3 * PAIRS)
+    early = exchange(early)
+    late, sums = columns(second, params, 0, 3 * PAIRS, sums, late)
+    late = exchange(late)
+    done = unpack(early, 0, structs, ())
+    done = unpack(late, 1, structs, tuple(done))
+    totals = all_sum(sums)
     matrices = jnp.concatenate(
         [totals[:160].reshape(5 * HD, 128), totals[160:320].reshape(5 * HD, 128)], axis=1
     ).reshape(5, HD, C)

time: 285 us -> 276 us (0.968)
  the two profiles are of different devices: /device:TPU:32 before, /device:TPU:1 now
where the time goes in v2:
time: 276 us; the launch traced here: 275 us
  waiting for transfers between devices  102 us (37%)
  starting transfers between devices  72.8 us (26%)
  Pallas kernels  66 us (24%)
  local copies, waits for them, and re-layouts  27.4 us (10%)
  other arithmetic  5.36 us (2%)
    pallas_call x2, Pallas kernels, columns(): pl.pallas_call(functools.partial(pair_kernel, pairs, early, bool(later)),...  52.4 us
    all_to_all x4, waiting for transfers between devices, exchange(): return lax.all_to_all(value, DAP, 0, 0, tiled=True)  46.2 us
    all_to_all x4, starting transfers between devices, exchange(): return lax.all_to_all(value, DAP, 0, 0, tiled=True)  37.9 us
    ppermute x3, waiting for transfers between devices, swap_sum(): lax.ppermute(value, axis, [(k, k ^ bit) for k in range(size)])  32.5 us
    ppermute x14, starting transfers between devices, shift(): lax.ppermute(value, axes, [(k, (k + step) % size) for k in range(size)])  26.1 us
    ppermute x14, waiting for transfers between devices, shift(): lax.ppermute(value, axes, [(k, (k + step) % size) for k in range(size)])  23.5 us
    unnamed x46, local copies, waits for them, and re-layouts  10.8 us
    ppermute x3, starting transfers between devices, swap_sum(): lax.ppermute(value, axis, [(k, k ^ bit) for k in range(size)])  8.77 us
  transfers between devices with their start and end apart: 21, of which 14 were waited for; matrix products, arithmetic and copies ran while one was open for 8% of the time, Pallas kernels for 21%

profile of v2, /device:TPU:1, one launch (start us, length us, event | category | flops | bytes accessed | tf_op | source)
XLA Modules:
  0.0 274.6 jit_solution(2792134274046417615)
XLA Ops:
  0.6 4.3 %shard_map.147 = bf16[16,2,8,16,256]{4,3,2,1,0:T(8,128)(2,1)} custom-call(bf16[2,8,256,256]{3,2,1,0:T(8,128)(2,1)} %x_ref.3, bf16[2,8,256,256]{3,2,1,0:T(8,128)(2,1)} %cot_ref.3), custom_call_target="tpu_custom_call" | custom-call | bytes 4194304 | tf_op jit(solution)/shard_map/pallas_call | solution.py:64
  4.9 9.0 %all-to-all-start.1 = ((bf16[16,2,8,16,256]{4,3,2,1,0:T(8,128)(2,1)}), bf16[16,2,8,16,256]{4,3,2,1,0:T(8,128)(2,1)S(1)}, u32[]{:S(2)}, u32[]{:S(2)}) async-start(bf16[16,2,8,16,256]{4,3,2,1,0:T(8,128)(2,1)} %shard_map.147), calls=%async_computation.1 | async-start | bytes 4194304 | tf_op jit(solution)/shard_map/all_to_all | solution.py:340
  14.0 4.3 %shard_map.146 = bf16[16,2,8,16,256]{4,3,2,1,0:T(8,128)(2,1)} custom-call(bf16[2,8,256,256]{3,2,1,0:T(8,128)(2,1)} %x_ref.3, bf16[2,8,256,256]{3,2,1,0:T(8,128)(2,1)} %cot_ref.3), custom_call_target="tpu_custom_call" | custom-call | bytes 4194304 | tf_op jit(solution)/shard_map/pallas_call | solution.py:64
  18.3 37.1 %all-to-all-done.1.refs_0_.refs_1_ = bf16[16,2,8,16,256]{4,3,2,1,0:T(8,128)(2,1)S(1)} async-done(((bf16[16,2,8,16,256]{4,3,2,1,0:T(8,128)(2,1)}), bf16[16,2,8,16,256]{4,3,2,1,0:T(8,128)(2,1)S(1)}, u32[]{:S(2)}, u32[]{:S(2)}) %all-to-all-start.1) | async-done | bytes 2097184 | tf_op jit(solution)/shard_map/all_to_all | solution.py:340
  56.7 11.0 %all-to-all-start = ((bf16[16,2,8,16,256]{4,3,2,1,0:T(8,128)(2,1)}), bf16[16,2,8,16,256]{4,3,2,1,0:T(8,128)(2,1)S(1)}, u32[]{:S(2)}, u32[]{:S(2)}) async-start(bf16[16,2,8,16,256]{4,3,2,1,0:T(8,128)(2,1)} %shard_map.146), calls=%async_computation | async-start | bytes 4194304 | tf_op jit(solution)/shard_map/all_to_all | solution.py:340
  70.9 1.6 copy-done.3
  72.5 26.6 %shard_map.148 = (bf16[16,2,4,16,256]{4,3,2,1,0:T(8,128)(2,1)}, bf16[16,2,12,16,256]{4,3,2,1,0:T(8,128)(2,1)}, f32[352,8,128]{2,1,0:T(8,128)S(1)}) custom-call(bf16[16,2,8,16,256]{4,3,2,1,0:T(8,128)(2,1)S(1)} %copy-done.3, bf16[16,2,8,16,256]{4,3,2,1,0:T(8,128)(2,1)S(1)} %copy-done.3, bf16[256,1024]{1,0:T(8,128)(2,1)S(1)} %copy.24.refs_2_, ...), custom_call_target="tpu_custom_call" | custom-call | flops 32000000000 | bytes 8388608 | tf_op jit(solution)/shard_map/pallas_call | solution.py:266
  100.1 9.1 %all-to-all-done.refs_0_.refs_1_ = bf16[16,2,8,16,256]{4,3,2,1,0:T(8,128)(2,1)S(1)} async-done(((bf16[16,2,8,16,256]{4,3,2,1,0:T(8,128)(2,1)}), bf16[16,2,8,16,256]{4,3,2,1,0:T(8,128)(2,1)S(1)}, u32[]{:S(2)}, u32[]{:S(2)}) %all-to-all-start) | async-done | bytes 2097184 | tf_op jit(solution)/shard_map/all_to_all | solution.py:340
  109.2 11.0 %all-to-all-start.3 = ((bf16[16,2,4,16,256]{4,3,2,1,0:T(8,128)(2,1)}), bf16[16,2,4,16,256]{4,3,2,1,0:T(8,128)(2,1)S(1)}, u32[]{:S(2)}, u32[]{:S(2)}) async-start(bf16[16,2,4,16,256]{4,3,2,1,0:T(8,128)(2,1)} %get-tuple-element.17), calls=%async_computation.3 | async-start | bytes 2097152 | tf_op jit(solution)/shard_map/all_to_all | solution.py:340
  123.6 25.8 %shard_map.149 = (bf16[16,2,12,16,256]{4,3,2,1,0:T(8,128)(2,1)}, f32[352,8,128]{2,1,0:T(8,128)S(1)}) custom-call(bf16[16,2,8,16,256]{4,3,2,1,0:T(8,128)(2,1)S(1)} %all-to-all-done.refs_0_.refs_1_, bf16[16,2,8,16,256]{4,3,2,1,0:T(8,128)(2,1)S(1)} %all-to-all-done.refs_0_.refs_1_, bf16[256,1024]{1,0:T(8,128)(2,1)S(1)} %copy-done.8, ...), custom_call_target="tpu_custom_call", output_to_operand_aliasing={{0}: (8, {})} | custom-call | flops 32000000000 | bytes 8388608 | tf_op jit(solution)/shard_map/pallas_call | solution.py:266
  151.6 7.0 %all-to-all-start.2 = ((bf16[16,2,12,16,256]{4,3,2,1,0:T(8,128)(2,1)}), bf16[16,2,12,16,256]{4,3,2,1,0:T(8,128)(2,1)S(1)}, u32[]{:S(2)}, u32[]{:S(2)}) async-start(bf16[16,2,12,16,256]{4,3,2,1,0:T(8,128)(2,1)} %get-tuple-element.16), calls=%async_computation.2 | async-start | bytes 6291456 | tf_op jit(solution)/shard_map/all_to_all | solution.py:340
  158.5 2.0 constant_dynamic-slice_fusion.6
  160.6 2.5 collective-permute-start
  163.0 2.2 collective-permute-done
  168.2 2.7 collective-permute-start.3
  171.9 6.6 %collective-permute-done.3 = f32[44,8,128]{2,1,0:T(8,128)} collective-permute-done((f32[44,8,128]{2,1,0:T(8,128)}, f32[44,8,128]{2,1,0:T(8,128)}, u32[]{:S(2)}, u32[]{:S(2)}) %collective-permute-start.3) | collective-permute-done | bytes 180256 | tf_op jit(solution)/shard_map/ppermute | solution.py:292
  178.5 4.3 %collective-permute-done.1 = f32[44,8,128]{2,1,0:T(8,128)} collective-permute-done((f32[44,8,128]{2,1,0:T(8,128)S(1)}, f32[44,8,128]{2,1,0:T(8,128)}, u32[]{:S(2)}, u32[]{:S(2)}) %collective-permute-start.1) | collective-permute-done | bytes 180256 | tf_op jit(solution)/shard_map/ppermute | solution.py:292
  184.7 2.8 %collective-permute-start.6 = (f32[11,8,128]{2,1,0:T(8,128)}, f32[11,8,128]{2,1,0:T(8,128)S(1)}, u32[]{:S(2)}, u32[]{:S(2)}) collective-permute-start(f32[11,8,128]{2,1,0:T(8,128)} %get-tuple-element.33), channel_id=1, source_target_pairs={{0,3},{1,0},{2,1},{3,2},{4,7},{5,4},{6,5},{7,6},{8,11},{9,8},{10,9... | collective-permute-start | bytes 135176 | tf_op jit(solution)/shard_map/ppermute | solution.py:292
  188.7 3.8 %collective-permute-done.6 = f32[11,8,128]{2,1,0:T(8,128)S(1)} collective-permute-done((f32[11,8,128]{2,1,0:T(8,128)}, f32[11,8,128]{2,1,0:T(8,128)S(1)}, u32[]{:S(2)}, u32[]{:S(2)}) %collective-permute-start.6) | collective-permute-done | bytes 45088 | tf_op jit(solution)/shard_map/ppermute | solution.py:292
  192.7 3.3 %collective-permute-done.4 = f32[11,8,128]{2,1,0:T(8,128)S(1)} collective-permute-done((f32[11,8,128]{2,1,0:T(8,128)S(1)}, f32[11,8,128]{2,1,0:T(8,128)S(1)}, u32[]{:S(2)}, u32[]{:S(2)}) %collective-permute-start.4) | collective-permute-done | bytes 45088 | tf_op jit(solution)/shard_map/ppermute | solution.py:292
  196.3 11.8 %collective-permute-done.7 = f32[11,8,128]{2,1,0:T(8,128)S(1)} collective-permute-done((f32[11,8,128]{2,1,0:T(8,128)S(1)}, f32[11,8,128]{2,1,0:T(8,128)S(1)}, u32[]{:S(2)}, u32[]{:S(2)}) %collective-permute-start.7) | collective-permute-done | bytes 45088 | tf_op jit(solution)/shard_map/ppermute | solution.py:318
  208.1 4.2 %collective-permute-start.8 = (f32[11,8,128]{2,1,0:T(8,128)S(1)}, f32[11,8,128]{2,1,0:T(8,128)S(1)}, u32[]{:S(2)}, u32[]{:S(2)}) collective-permute-start(f32[11,8,128]{2,1,0:T(8,128)S(1)} %add.158), channel_id=1, source_target_pairs={{0,8},{4,12},{8,0},{12,4},{1,9},{5,13},{9,1},{13,5},{2,10},{6,14},... | collective-permute-start | bytes 135176 | tf_op jit(solution)/shard_map/ppermute | solution.py:318
  212.3 18.0 %collective-permute-done.8 = f32[11,8,128]{2,1,0:T(8,128)S(1)} collective-permute-done((f32[11,8,128]{2,1,0:T(8,128)S(1)}, f32[11,8,128]{2,1,0:T(8,128)S(1)}, u32[]{:S(2)}, u32[]{:S(2)}) %collective-permute-start.8) | collective-permute-done | bytes 45088 | tf_op jit(solution)/shard_map/ppermute | solution.py:318
  230.3 4.2 %collective-permute-start.9 = (f32[11,8,128]{2,1,0:T(8,128)S(1)}, f32[11,8,128]{2,1,0:T(8,128)S(1)}, u32[]{:S(2)}, u32[]{:S(2)}) collective-permute-start(f32[11,8,128]{2,1,0:T(8,128)S(1)} %add.159), channel_id=1, source_target_pairs={{0,128},{128,0},{1,129},{129,1},{2,130},{130,2},{3,131},{131,3},{4... | collective-permute-start | bytes 135176 | tf_op jit(solution)/shard_map/ppermute | solution.py:318
  234.5 2.7 collective-permute-done.9
  238.5 2.7 collective-permute-start.11
  245.4 2.6 collective-permute-start.14
  251.3 1.5 collective-permute-done.14
  254.2 5.8 %collective-permute-start.16 = (f32[176,8,128]{2,1,0:T(8,128)}, f32[176,8,128]{2,1,0:T(8,128)}, u32[]{:S(2)}, u32[]{:S(2)}) collective-permute-start(f32[176,8,128]{2,1,0:T(8,128)} %constant_dynamic-update-slice_fusion.2), channel_id=1, source_target_pairs={{0,16},{16,0},{1,17},{17,1},{2,18},{18,2},{3,19},{19,3},{4,20},{20... | collective-permute-start | bytes 2162696 | tf_op jit(solution)/shard_map/ppermute | solution.py:292
  261.1 2.0 constant_dynamic-update-slice_fusion.1
  264.5 2.0 constant_dynamic-update-slice_fusion
  271.0 3.7 %shard_map.151 = (bf16[2,8,256,256]{3,2,1,0:T(8,128)(2,1)}, bf16[2,8,256,256]{3,2,1,0:T(8,128)(2,1)}) custom-call(bf16[16,2,12,16,256]{4,3,2,1,0:T(8,128)(2,1)S(1)} %all-to-all-done.2.refs_0_, bf16[2,8,256,256]{3,2,1,0:T(8,128)(2,1)} %get-tuple-element.18.refs_1_, ...), custom_call_target="tpu_custom_call", output_to_operand_aliasing={{0}: (1, {}), {1}: (2, {})} | custom-call | bytes 6291456 | tf_op jit(solution)/shard_map/pallas_call | solution.py:92
  (94 shorter events, 35.7 us)
Async XLA Ops:
  4.9 50.5 %all-to-all-start.1 = ((bf16[16,2,8,16,256]{4,3,2,1,0:T(8,128)(2,1)}), bf16[16,2,8,16,256]{4,3,2,1,0:T(8,128)(2,1)S(1)}, u32[]{:S(2)}, u32[]{:S(2)}) async-start(bf16[16,2,8,16,256]{4,3,2,1,0:T(8,128)(2,1)} %shard_map.147), calls=%async_computation.1 | async-start | bytes 4194304 | tf_op jit(solution)/shard_map/all_to_all | solution.py:340
  18.3 49.5 %copy-start.13 = (bf16[256,256]{1,0:T(8,128)(2,1)S(1)}, bf16[256,256]{1,0:T(8,128)(2,1)}, u32[]{:S(2)}) copy-start(bf16[256,256]{1,0:T(8,128)(2,1)} %param.16) | copy-start | bytes 393220
  18.3 49.6 %copy-start.14 = (bf16[256,256]{1,0:T(8,128)(2,1)S(1)}, bf16[256,256]{1,0:T(8,128)(2,1)}, u32[]{:S(2)}) copy-start(bf16[256,256]{1,0:T(8,128)(2,1)} %param.15) | copy-start | bytes 393220
  18.3 49.7 %copy-start.15 = (bf16[256,256]{1,0:T(8,128)(2,1)S(1)}, bf16[256,256]{1,0:T(8,128)(2,1)}, u32[]{:S(2)}) copy-start(bf16[256,256]{1,0:T(8,128)(2,1)} %param.14) | copy-start | bytes 393220
  18.3 49.8 %copy-start.16 = (bf16[256,256]{1,0:T(8,128)(2,1)S(1)}, bf16[256,256]{1,0:T(8,128)(2,1)}, u32[]{:S(2)}) copy-start(bf16[256,256]{1,0:T(8,128)(2,1)} %param.13) | copy-start | bytes 393220
  56.7 52.5 %all-to-all-start = ((bf16[16,2,8,16,256]{4,3,2,1,0:T(8,128)(2,1)}), bf16[16,2,8,16,256]{4,3,2,1,0:T(8,128)(2,1)S(1)}, u32[]{:S(2)}, u32[]{:S(2)}) async-start(bf16[16,2,8,16,256]{4,3,2,1,0:T(8,128)(2,1)} %shard_map.146), calls=%async_computation | async-start | bytes 4194304 | tf_op jit(solution)/shard_map/all_to_all | solution.py:340
  68.1 2.6 copy-start.18
  68.1 2.6 copy-start.19
  68.1 2.6 copy-start.17
  68.3 2.6 copy-start.9
  69.1 29.9 %copy-start.5 = (bf16[1024,256]{1,0:T(8,128)(2,1)}, bf16[1024,256]{1,0:T(8,128)(2,1)S(1)}, u32[]{:S(2)}) copy-start(bf16[1024,256]{1,0:T(8,128)(2,1)S(1)} %get-tuple-element.30.refs_3_) | copy-start | bytes 1572868
  70.6 28.5 %copy-start.7 = (bf16[256,1024]{1,0:T(8,128)(2,1)}, bf16[256,1024]{1,0:T(8,128)(2,1)S(1)}, u32[]{:S(2)}) copy-start(bf16[256,1024]{1,0:T(8,128)(2,1)S(1)} %copy.24.refs_2_) | copy-start | bytes 1572868
  109.2 41.4 %all-to-all-start.3 = ((bf16[16,2,4,16,256]{4,3,2,1,0:T(8,128)(2,1)}), bf16[16,2,4,16,256]{4,3,2,1,0:T(8,128)(2,1)S(1)}, u32[]{:S(2)}, u32[]{:S(2)}) async-start(bf16[16,2,4,16,256]{4,3,2,1,0:T(8,128)(2,1)} %get-tuple-element.17), calls=%async_computation.3 | async-start | bytes 2097152 | tf_op jit(solution)/shard_map/all_to_all | solution.py:340
  151.6 119.4 %all-to-all-start.2 = ((bf16[16,2,12,16,256]{4,3,2,1,0:T(8,128)(2,1)}), bf16[16,2,12,16,256]{4,3,2,1,0:T(8,128)(2,1)S(1)}, u32[]{:S(2)}, u32[]{:S(2)}) async-start(bf16[16,2,12,16,256]{4,3,2,1,0:T(8,128)(2,1)} %get-tuple-element.16), calls=%async_computation.2 | async-start | bytes 6291456 | tf_op jit(solution)/shard_map/all_to_all | solution.py:340
  160.6 4.6 %collective-permute-start = (f32[176,8,128]{2,1,0:T(8,128)}, f32[176,8,128]{2,1,0:T(8,128)}, u32[]{:S(2)}, u32[]{:S(2)}) collective-permute-start(f32[176,8,128]{2,1,0:T(8,128)} %constant_dynamic-slice_fusion.6), channel_id=1, source_target_pairs={{0,16},{16,0},{1,17},{17,1},{2,18},{18,2},{3,19},{19,3},{4,20},{20... | collective-permute-start | bytes 2162696 | tf_op jit(solution)/shard_map/ppermute | solution.py:292
  168.2 10.3 %collective-permute-start.3 = (f32[44,8,128]{2,1,0:T(8,128)}, f32[44,8,128]{2,1,0:T(8,128)}, u32[]{:S(2)}, u32[]{:S(2)}) collective-permute-start(f32[44,8,128]{2,1,0:T(8,128)} %get-tuple-element.28), channel_id=1, source_target_pairs={{0,96},{32,0},{64,32},{96,64},{1,97},{33,1},{65,33},{97,65},{2,98}... | collective-permute-start | bytes 540680 | tf_op jit(solution)/shard_map/ppermute | solution.py:292
  170.9 7.6 %collective-permute-start.2 = (f32[44,8,128]{2,1,0:T(8,128)S(1)}, f32[44,8,128]{2,1,0:T(8,128)}, u32[]{:S(2)}, u32[]{:S(2)}) collective-permute-start(f32[44,8,128]{2,1,0:T(8,128)S(1)} %get-tuple-element.29), channel_id=1, source_target_pairs={{0,64},{32,96},{64,0},{96,32},{1,65},{33,97},{65,1},{97,33},{2,66}... | collective-permute-start | bytes 540680 | tf_op jit(solution)/shard_map/ppermute | solution.py:292
  171.2 11.6 %collective-permute-start.1 = (f32[44,8,128]{2,1,0:T(8,128)S(1)}, f32[44,8,128]{2,1,0:T(8,128)}, u32[]{:S(2)}, u32[]{:S(2)}) collective-permute-start(f32[44,8,128]{2,1,0:T(8,128)S(1)} %get-tuple-element.27), channel_id=1, source_target_pairs={{0,32},{32,64},{64,96},{96,0},{1,33},{33,65},{65,97},{97,1},{2,34}... | collective-permute-start | bytes 540680 | tf_op jit(solution)/shard_map/ppermute | solution.py:292
  184.7 7.8 %collective-permute-start.6 = (f32[11,8,128]{2,1,0:T(8,128)}, f32[11,8,128]{2,1,0:T(8,128)S(1)}, u32[]{:S(2)}, u32[]{:S(2)}) collective-permute-start(f32[11,8,128]{2,1,0:T(8,128)} %get-tuple-element.33), channel_id=1, source_target_pairs={{0,3},{1,0},{2,1},{3,2},{4,7},{5,4},{6,5},{7,6},{8,11},{9,8},{10,9... | collective-permute-start | bytes 135176 | tf_op jit(solution)/shard_map/ppermute | solution.py:292
  187.5 5.1 %collective-permute-start.5 = (f32[11,8,128]{2,1,0:T(8,128)S(1)}, f32[11,8,128]{2,1,0:T(8,128)S(1)}, u32[]{:S(2)}, u32[]{:S(2)}) collective-permute-start(f32[11,8,128]{2,1,0:T(8,128)S(1)} %get-tuple-element.34), channel_id=1, source_target_pairs={{0,2},{1,3},{2,0},{3,1},{4,6},{5,7},{6,4},{7,5},{8,10},{9,11},{10,... | collective-permute-start | bytes 135176 | tf_op jit(solution)/shard_map/ppermute | solution.py:292
  188.1 7.8 %collective-permute-start.4 = (f32[11,8,128]{2,1,0:T(8,128)S(1)}, f32[11,8,128]{2,1,0:T(8,128)S(1)}, u32[]{:S(2)}, u32[]{:S(2)}) collective-permute-start(f32[11,8,128]{2,1,0:T(8,128)S(1)} %get-tuple-element.32), channel_id=1, source_target_pairs={{0,1},{1,2},{2,3},{3,0},{4,5},{5,6},{6,7},{7,4},{8,9},{9,10},{10,1... | collective-permute-start | bytes 135176 | tf_op jit(solution)/shard_map/ppermute | solution.py:292
  195.9 12.1 %collective-permute-start.7 = (f32[11,8,128]{2,1,0:T(8,128)S(1)}, f32[11,8,128]{2,1,0:T(8,128)S(1)}, u32[]{:S(2)}, u32[]{:S(2)}) collective-permute-start(f32[11,8,128]{2,1,0:T(8,128)S(1)} %add_add_fusion.1), channel_id=1, source_target_pairs={{0,4},{4,0},{8,12},{12,8},{1,5},{5,1},{9,13},{13,9},{2,6},{6,2},{1... | collective-permute-start | bytes 135176 | tf_op jit(solution)/shard_map/ppermute | solution.py:318
  208.1 22.2 %collective-permute-start.8 = (f32[11,8,128]{2,1,0:T(8,128)S(1)}, f32[11,8,128]{2,1,0:T(8,128)S(1)}, u32[]{:S(2)}, u32[]{:S(2)}) collective-permute-start(f32[11,8,128]{2,1,0:T(8,128)S(1)} %add.158), channel_id=1, source_target_pairs={{0,8},{4,12},{8,0},{12,4},{1,9},{5,13},{9,1},{13,5},{2,10},{6,14},... | collective-permute-start | bytes 135176 | tf_op jit(solution)/shard_map/ppermute | solution.py:318
  230.3 6.9 %collective-permute-start.9 = (f32[11,8,128]{2,1,0:T(8,128)S(1)}, f32[11,8,128]{2,1,0:T(8,128)S(1)}, u32[]{:S(2)}, u32[]{:S(2)}) collective-permute-start(f32[11,8,128]{2,1,0:T(8,128)S(1)} %add.159), channel_id=1, source_target_pairs={{0,128},{128,0},{1,129},{129,1},{2,130},{130,2},{3,131},{131,3},{4... | collective-permute-start | bytes 135176 | tf_op jit(solution)/shard_map/ppermute | solution.py:318
  237.2 5.1 %collective-permute-start.10 = (f32[11,8,128]{2,1,0:T(8,128)S(1)}, f32[11,8,128]{2,1,0:T(8,128)S(1)}, u32[]{:S(2)}, u32[]{:S(2)}) collective-permute-start(f32[11,8,128]{2,1,0:T(8,128)S(1)} %get-tuple-element.24), channel_id=1, source_target_pairs={{0,1},{1,2},{2,3},{3,0},{4,5},{5,6},{6,7},{7,4},{8,9},{9,10},{10,1... | collective-permute-start | bytes 135176 | tf_op jit(solution)/shard_map/ppermute | solution.py:292
  238.5 4.6 %collective-permute-start.11 = (f32[11,8,128]{2,1,0:T(8,128)S(1)}, f32[11,8,128]{2,1,0:T(8,128)S(1)}, u32[]{:S(2)}, u32[]{:S(2)}) collective-permute-start(f32[11,8,128]{2,1,0:T(8,128)S(1)} %get-tuple-element.24), channel_id=1, source_target_pairs={{0,2},{1,3},{2,0},{3,1},{4,6},{5,7},{6,4},{7,5},{8,10},{9,11},{10,... | collective-permute-start | bytes 135176 | tf_op jit(solution)/shard_map/ppermute | solution.py:292
  241.2 2.9 %collective-permute-start.12 = (f32[11,8,128]{2,1,0:T(8,128)S(1)}, f32[11,8,128]{2,1,0:T(8,128)S(1)}, u32[]{:S(2)}, u32[]{:S(2)}) collective-permute-start(f32[11,8,128]{2,1,0:T(8,128)S(1)} %get-tuple-element.24), channel_id=1, source_target_pairs={{0,3},{1,0},{2,1},{3,2},{4,7},{5,4},{6,5},{7,6},{8,11},{9,8},{10,9... | collective-permute-start | bytes 135176 | tf_op jit(solution)/shard_map/ppermute | solution.py:292
  244.1 6.6 %collective-permute-start.13 = (f32[44,8,128]{2,1,0:T(8,128)S(1)}, f32[44,8,128]{2,1,0:T(8,128)S(1)}, u32[]{:S(2)}, u32[]{:S(2)}) collective-permute-start(f32[44,8,128]{2,1,0:T(8,128)S(1)} %constant_dynamic-update-slice_fusion.6), channel_id=1, source_target_pairs={{0,32},{32,64},{64,96},{96,0},{1,33},{33,65},{65,97},{97,1},{2,34}... | collective-permute-start | bytes 540680 | tf_op jit(solution)/shard_map/ppermute | solution.py:292
  245.4 7.4 %collective-permute-start.14 = (f32[44,8,128]{2,1,0:T(8,128)S(1)}, f32[44,8,128]{2,1,0:T(8,128)S(1)}, u32[]{:S(2)}, u32[]{:S(2)}) collective-permute-start(f32[44,8,128]{2,1,0:T(8,128)S(1)} %constant_dynamic-update-slice_fusion.6), channel_id=1, source_target_pairs={{0,64},{32,96},{64,0},{96,32},{1,65},{33,97},{65,1},{97,33},{2,66}... | collective-permute-start | bytes 540680 | tf_op jit(solution)/shard_map/ppermute | solution.py:292
  248.0 5.5 %collective-permute-start.15 = (f32[44,8,128]{2,1,0:T(8,128)S(1)}, f32[44,8,128]{2,1,0:T(8,128)S(1)}, u32[]{:S(2)}, u32[]{:S(2)}) collective-permute-start(f32[44,8,128]{2,1,0:T(8,128)S(1)} %constant_dynamic-update-slice_fusion.6), channel_id=1, source_target_pairs={{0,96},{32,0},{64,32},{96,64},{1,97},{33,1},{65,33},{97,65},{2,98}... | collective-permute-start | bytes 540680 | tf_op jit(solution)/shard_map/ppermute | solution.py:292
  254.2 10.3 %collective-permute-start.16 = (f32[176,8,128]{2,1,0:T(8,128)}, f32[176,8,128]{2,1,0:T(8,128)}, u32[]{:S(2)}, u32[]{:S(2)}) collective-permute-start(f32[176,8,128]{2,1,0:T(8,128)} %constant_dynamic-update-slice_fusion.2), channel_id=1, source_target_pairs={{0,16},{16,0},{1,17},{17,1},{2,18},{18,2},{3,19},{19,3},{4,20},{20... | collective-permute-start | bytes 2162696 | tf_op jit(solution)/shard_map/ppermute | solution.py:292
  259.9 3.2 %copy-start.1 = (bf16[16,2,4,16,256]{4,3,2,1,0:T(8,128)(2,1)S(1)}, bf16[16,2,4,16,256]{4,3,2,1,0:T(8,128)(2,1)}, u32[]{:S(2)}) copy-start(bf16[16,2,4,16,256]{4,3,2,1,0:T(8,128)(2,1)} %copy-done) | copy-start | bytes 3145732
  (10 other events, 12.9 us)
